TPU v7x, 256 devices: a whole 4x4x8 slice. The times are simulated.
256 devices in a mesh: dom: 4 (over x), gx: 16 (over z, y_hi), gy: 4 (over y_lo, core).
Axes of the slice: x: 4, y: 4 (y_hi: 2, y_lo: 2; y = y_hi * 2 + y_lo), z: 8, core: 2. Of those that a mesh axis runs over, the one named last changes fastest.
Arguments:
- state: float32 [9, 32, 128, 1024], P(None, 'dom', 'gx', 'gy'), may hold values from -6 to 6
- source: float32 [6, 128, 1024], P(None, 'gx', 'gy'), may hold values from -6 to 6
- seafloor: int32 [128, 1024], P('gx', 'gy'), may hold values from 1 to 8
- region: int32 [32, 128, 1024], P('dom', 'gx', 'gy'), may hold values from 0 to 15
- lame_lambda: float32 [16], replicated, may hold values from 1 to 2
- shear_mu: float32 [16], replicated, may hold values from 0.3 to 0.6
- buoyancy: float32 [16], replicated, may hold values from 0.5 to 1
Outputs:
- adjoint_state: float32 [9, 32, 128, 1024], P(None, 'dom', 'gx', 'gy')
All inputs are finite; a program needn't handle non-finite values.
Results may differ from a plain program's by a relative error of at most 0.00011.
Values sent between devices are 32-bit elements; how exact they have to be, the bound alone decides.
A program may use at most 64 MiB of HBM per device.

v0:
```python
import functools

import jax
import jax.numpy as jnp
from jax import lax
from jax.experimental import pallas as pl
from jax.experimental.pallas import tpu as pltpu
from jax.sharding import PartitionSpec as P

STEPS = 6
COURANT = 0.25
REGIONS = 16
BLOCK = 16
WIDE = 12
MIDDLE, LEFT, RIGHT = 0, 1, 2
FIRST_CUT, SECOND_CUT, SEAM = 86, 171 - 128, 64
MESH = pl.DeviceIdType.MESH

f32 = jnp.float32


def rows(z, x=0):
    return (z + 1) * BLOCK + 8 + x


def level(z):
    return pl.ds(rows(z), 8)


def column(x):
    return pl.ds(rows(0, x), 8, stride=BLOCK)


def dy(v):
    return pltpu.roll(v, 127, 1) - pltpu.roll(v, 1, 1)


def pick(bits, table):
    values = list(table)
    for bit in bits:
        values = [jnp.where(bit, values[2 * i + 1], values[2 * i]) for i in range(len(values) // 2)]
    return values[0]


def kernel(
    sizes, state_in, source_in, floor_in, region_in, lame_in, shear_in, buoy_in, out,
    state, source, floor, region, lame, shear, buoy,
    S, V, L, M, B, SRC, LX, MX, SX, LZ, MZ, OX, OZ, OE, XR0, ZR0, YR, XR, ZR, ER,
    in_sem, x_send, z_send, e_send, x_first_recv, z_first_recv, y_recv, x_recv, z_recv, e_recv,
):
    n_dom, n_gx, n_gy = sizes
    dom, gx, gy = lax.axis_index("dom"), lax.axis_index("gx"), lax.axis_index("gy")
    lane = lax.broadcasted_iota(jnp.int32, (8, 128), 1)
    sub = lax.broadcasted_iota(jnp.int32, (8, 128), 0)
    zero = jnp.zeros((8, 128), f32)

    loads = [
        pltpu.make_async_copy(src, dst, in_sem.at[i])
        for i, (src, dst) in enumerate((
            (region_in, region), (floor_in, floor), (source_in, source), (state_in, state),
            (lame_in, lame), (shear_in, shear), (buoy_in, buoy)))
    ]
    for load in loads:
        load.start()

    sides = (-1, 1)
    there = [gx > 0, gx < n_gx - 1]
    z_there = [dom > 0, dom < n_dom - 1]

    doms = [dom, jnp.where(dom == n_dom - 1, 0, dom + 1), jnp.where(dom == 0, n_dom - 1, dom - 1)]
    gxs = [gx, gx + 1, gx - 1]
    gys = [gy, jnp.where(gy == n_gy - 1, 0, gy + 1), jnp.where(gy == 0, n_gy - 1, gy - 1)]

    def at(dz, dx, dyy):
        return (doms[dz], gxs[dx], gys[dyy])

    def reach(i, then):
        pl.when(there[i])(then)

    barrier = pltpu.get_barrier_semaphore()

    def greet(*way):
        pl.semaphore_signal(barrier, inc=1, device_id=at(*way), device_id_type=MESH)

    for i, dx in enumerate(sides):
        @functools.partial(reach, i)
        def _(dx=dx):
            for way in ((0, dx, 0), (-1, dx, 0), (1, dx, 0), (0, dx, -1), (0, dx, 1)):
                greet(*way)
    for way in [(a, 0, b) for a in (-1, 0, 1) for b in (-1, 0, 1) if a or b]:
        greet(*way)

    for i in range(2):
        @pl.when(jnp.logical_not(there[i]))
        def _(i=i):
            XR0[i] = jnp.zeros(XR0.shape[1:], f32)
            for slot in range(2):
                for p in range(3):
                    XR[slot, p, i] = jnp.zeros(XR.shape[3:], f32)
                    ER[slot, p, i] = jnp.zeros(ER.shape[3:], f32)

    for p in range(3):
        for f in range(3):
            for z in range(-1, 9):
                V[p, f, pl.ds(rows(z, -8), 8), :] = zero
            for z in (-1, 8):
                V[p, f, level(z), :] = zero

    for load in loads[:4]:
        load.wait()

    def side_by_side(parts, t):
        tile = zero
        for k, v in enumerate(parts):
            shift = (WIDE * k + (WIDE if t else 0)) % 128
            v = pltpu.roll(v, shift, 1) if shift else v
            tile = jnp.where((lane >= WIDE * k) & (lane < WIDE * (k + 1)), v, tile)
        return tile

    def cut(t):
        return slice(128 * t, 128 * t + 128)

    for i in range(2):
        for z in range(8):
            OZ[i, 111 + z] = side_by_side(
                [state[f, z, :, cut(i)] for f in range(9)] + [region[z, :, cut(i)].astype(f32)], i)
        OZ[i, 119] = side_by_side([source[s, :, cut(i)] for s in range(STEPS)] + [floor[:, cut(i)].astype(f32)], i)

    def remote(src, dst, send, recv, way):
        return pltpu.make_async_remote_copy(
            src_ref=src, dst_ref=dst, send_sem=send, recv_sem=recv, device_id=at(*way), device_id_type=MESH)

    def xa_first(i):
        return remote(OX.at[i, 0:6], XR0.at[1 - i, 0:6], x_send.at[i], x_first_recv.at[0, 1 - i], (0, sides[i], 0))

    def xy_first(i, j):
        return remote(
            OX.at[i, 6 + j], XR0.at[1 - i, 7 - j], x_send.at[i], x_first_recv.at[0, 1 - i], (0, sides[i], sides[j]))

    def xb_first(i):
        return remote(OX.at[i, 8:14], XR0.at[1 - i, 8:14], x_send.at[i], x_first_recv.at[1, 1 - i], (0, sides[i], 0))

    def za_first(i):
        return remote(OZ.at[i, 0:6], ZR0.at[1 - i, 0:6], z_send.at[i], z_first_recv.at[0], (sides[i], 0, 0))

    def zy_first(i, j):
        return remote(
            OZ.at[i, 6 + j], ZR0.at[1 - i, 7 - j], z_send.at[i], z_first_recv.at[0], (sides[i], 0, sides[j]))

    def zb_first(i):
        return remote(OZ.at[i, 8:12], ZR0.at[1 - i, 8:12], z_send.at[i], z_first_recv.at[1], (sides[i], 0, 0))

    def y_first(i):
        return remote(OZ.at[i, 111:120], YR.at[1 - i], z_send.at[i], y_recv.at[0], (0, 0, sides[i]))

    def arrived(ref, sem):
        pltpu.make_async_copy(ref, ref, sem).wait()

    for load in loads[4:]:
        load.wait()
    scale = 0.5 * COURANT
    tables = [[t[k] * scale for k in range(REGIONS)] for t in (lame, shear, buoy)]

    def materials(number, seafloor, z):
        bits = [(number & (1 << k)) != 0 for k in range(4)]
        solid = (dom * 8 + z) >= seafloor
        lam, mu, b = (pick(bits, t) for t in tables)
        return lam, jnp.where(solid, mu, 0.0), b, solid

    def put(ref, index, pair):
        ref[(MIDDLE, *index)] = jnp.where(lane < SEAM, pair[1], pair[0])
        ref[(LEFT, *index)] = pair[0]
        ref[(RIGHT, *index)] = pair[1]

    def put_margin(ref, index, v):
        ref[(LEFT, *index)] = jnp.where(lane >= 128 - WIDE, v, ref[(LEFT, *index)])
        ref[(RIGHT, *index)] = jnp.where(lane < WIDE, v, ref[(RIGHT, *index)])

    everywhere = slice(None)
    for s in range(STEPS):
        put(SRC, (pl.ds(8 * s, 8), everywhere),
            [jnp.where(dom == 0, source[s, :, cut(t)], 0.0) for t in range(2)])
    for z in range(8):
        made = [materials(region[z, :, cut(t)], floor[:, cut(t)], z) for t in range(2)]
        for k, ref in enumerate((L, M, B)):
            put(ref, (pl.ds(8 * z, 8), everywhere), [m[k] for m in made])
        for f in range(9):
            v = [state[f, z, :, cut(t)] for t in range(2)]
            if f < 3:
                put(V, (f, level(z), everywhere), v)
            else:
                if f >= 6:
                    v = [jnp.where(m[3], w, 0.0) for m, w in zip(made, v)]
                elif z == 0:
                    v = [w + jnp.where(dom == 0, source[0, :, cut(t)], 0.0) for t, w in enumerate(v)]
                put(S, (f - 3, level(z), everywhere), v)

    x_fields, z_fields = (0, 3, 4), (2, 4, 5)
    pair = (LEFT, RIGHT)
    for i, x in ((0, 0), (1, 7)):
        parts = [[S[p, f, column(x), :] for p in pair] for f in x_fields]
        parts += [[m[p, pl.ds(x, 8, stride=8), :] for p in pair] for m in (L, M)]
        parts += [[
            jnp.concatenate([SRC[p, pl.ds(x, STEPS, stride=8), :], jnp.zeros((8 - STEPS, 128), f32)], 0) for p in pair]]
        for k in range(6):
            for t in range(2):
                OX[i, 2 * k + t + (0 if k < 3 else 2)] = parts[k][t]
        for j in range(2):
            OX[i, 6 + j] = side_by_side([v[j] for v in parts], j)
    for i, z in ((0, 0), (1, 7)):
        parts = [[S[p, f, level(z), :] for p in pair] for f in z_fields]
        parts += [[m[p, pl.ds(8 * z, 8), :] for p in pair] for m in (L, M)]
        for k in range(5):
            for t in range(2):
                OZ[i, 2 * k + t + (0 if k < 3 else 2)] = parts[k][t]
        for j in range(2):
            OZ[i, 6 + j] = side_by_side([v[j] for v in parts], j)

    pl.semaphore_wait(barrier, 8 + 5 * (there[0].astype(jnp.int32) + there[1].astype(jnp.int32)))
    for i in range(2):
        @functools.partial(reach, i)
        def _(i=i):
            xa_first(i).start()
            for j in range(2):
                xy_first(i, j).start()
    for i in range(2):
        y_first(i).start()
        za_first(i).start()
        for j in range(2):
            zy_first(i, j).start()
    for i in range(2):
        @functools.partial(reach, i)
        def _(i=i):
            xb_first(i).start()
        zb_first(i).start()

    left = (lane >= 128 - WIDE) & (gy > 0)
    right = (lane < WIDE) & (gy < n_gy - 1)
    inside = left | right

    def margin(low, high, f):
        shift_r = (128 - WIDE * f) % 128
        shift_l = (256 - WIDE - WIDE * f) % 128
        a = pltpu.roll(high, shift_r, 1) if shift_r else high
        c = pltpu.roll(low, shift_l, 1) if shift_l else low
        return jnp.where(left, c, jnp.where(right, a, 0.0))

    arrived(ZR0.at[:, 0:8], z_first_recv.at[0])
    for i in range(2):
        @functools.partial(reach, i)
        def _(i=i):
            arrived(XR0.at[i, 0:8], x_first_recv.at[0, i])

    def three(first_tile, second_tile, edge):
        return (
            jnp.where(lane < SEAM, second_tile, first_tile),
            jnp.where(lane >= 128 - WIDE, edge, first_tile),
            jnp.where(lane < WIDE, edge, second_tile),
        )

    def border(parts):
        for i, x in ((0, -1), (1, 8)):
            for k, f in enumerate(x_fields):
                edge = zero if parts == (MIDDLE,) else margin(XR0[i, 6], XR0[i, 7], k)
                tiles = three(XR0[i, 2 * k], XR0[i, 2 * k + 1], edge)
                for p in parts:
                    S[p, f, column(x), :] = tiles[p]
        for i, z in ((0, -1), (1, 8)):
            for k, f in enumerate(z_fields):
                edge = zero if parts == (MIDDLE,) else margin(ZR0[i, 6], ZR0[i, 7], k)
                tiles = three(ZR0[i, 2 * k], ZR0[i, 2 * k + 1], edge)
                for p in parts:
                    S[p, f, level(z), :] = jnp.where(z_there[i], tiles[p], 0.0)

    border((MIDDLE,))
    def x_base(p, s, last):
        return 14 + 18 * s + (3 * p if last else 6 * p)

    def z_base(p, s, last):
        return 12 + 18 * s + (3 * p if last else 6 * p)

    def x_copy(p, i, s, slot, last):
        n = 3 if last else 6
        return remote(
            OX.at[i, pl.ds(x_base(p, s, last), n)], XR.at[slot, p, 1 - i, 0:n], x_send.at[i], x_recv.at[slot, p, 1 - i],
            (0, sides[i], 0))

    def e_copy(p, i, j, s, slot):
        return remote(
            OE.at[i, 3 * s + p, j], ER.at[slot, p, 1 - i, 1 - j], e_send.at[i],
            e_recv.at[slot, p, 1 - i], (sides[j], sides[i], 0))

    def z_copy(p, i, s, slot, last):
        n = 3 if last else 6
        return remote(
            OZ.at[i, pl.ds(z_base(p, s, last), n)], ZR.at[slot, p, 1 - i, 0:n], z_send.at[i], z_recv.at[slot, p],
            (sides[i], 0, 0))

    def move(p, s, slot, begin=False, last=False):
        if not begin:
            at_step = pl.ds(8 * s if last else pl.multiple_of(8 * s, 8), 8)
            added = SRC[p, at_step, :]
            for f in range(3):
                S[p, f, level(0), :] += added
            for i, x in ((0, -1), (1, 8)):
                S[p, 0, pl.ds(rows(0, x), 1), :] += SX[i, p, pl.ds(s, 1), :]

        def accelerate(z):
            own = level(z)
            after, before = pl.ds(rows(z, 1), 8), pl.ds(rows(z, -1), 8)
            above, below = level(z + 1), level(z - 1)

            def dx(f):
                return S[p, f, after, :] - S[p, f, before, :]

            def dz(f):
                return S[p, f, above, :] - S[p, f, below, :]

            b = B[p, pl.ds(8 * z, 8), :]
            V[p, 0, own, :] -= b * (dx(0) + dy(S[p, 3, own, :]) + dz(4))
            V[p, 1, own, :] -= b * (dx(3) + dy(S[p, 1, own, :]) + dz(5))
            V[p, 2, own, :] -= b * (dx(4) + dy(S[p, 5, own, :]) + dz(2))

        for z in (0, 7):
            accelerate(z)
        if not last:
            for i, x in ((0, 0), (1, 7)):
                for j in range(2):
                    for k, f in enumerate((0, 2)):
                        OE[i, 3 * s + p, j, k : k + 1, :] = V[p, f, pl.ds(rows(7 * j, x), 1), :]

                @functools.partial(reach, i)
                def _(i=i):
                    for j in range(2):
                        e_copy(p, i, j, s, slot).start()
        for z in range(1, 7):
            accelerate(z)
        base = x_base(p, s, last)
        for i, (x, inner) in enumerate(((0, 1), (7, 6))):
            for f in range(3):
                OX[i, base + f] = V[p, f, column(x), :]
                if not last:
                    OX[i, base + 3 + f] = V[p, f, column(inner), :]

            @functools.partial(reach, i)
            def _(i=i):
                x_copy(p, i, s, slot, last).start()
        base = z_base(p, s, last)
        for i, (z, inner) in enumerate(((0, 1), (7, 6))):
            for f in range(3):
                OZ[i, base + f] = V[p, f, level(z), :]
                if not last:
                    OZ[i, base + 3 + f] = V[p, f, level(inner), :]
            z_copy(p, i, s, slot, last).start()

        for z in range(8):
            own = level(z)
            after, before = pl.ds(rows(z, 1), 8), pl.ds(rows(z, -1), 8)
            above, below = level(z + 1), level(z - 1)
            dxs = [V[p, f, after, :] - V[p, f, before, :] for f in range(3)]
            dzs = [V[p, f, above, :] - V[p, f, below, :] for f in range(3)]
            dys = [dy(V[p, f, own, :]) for f in range(3)]
            lam, mu = L[p, pl.ds(8 * z, 8), :], M[p, pl.ds(8 * z, 8), :]
            spread = lam * (dxs[0] + dys[1] + dzs[2])
            mu2 = mu + mu
            S[p, 0, own, :] -= spread + mu2 * dxs[0]
            S[p, 1, own, :] -= spread + mu2 * dys[1]
            S[p, 2, own, :] -= spread + mu2 * dzs[2]
            S[p, 3, own, :] -= mu * (dys[0] + dxs[1])
            S[p, 4, own, :] -= mu * (dzs[0] + dxs[2])
            S[p, 5, own, :] -= mu * (dzs[1] + dys[2])

    def finish(p, slot, last=False):
        arrived(ZR.at[slot, p, :, 0:3] if last else ZR.at[slot, p], z_recv.at[slot, p])
        for i, z in ((0, 0), (1, 7)):
            near = [ZR[slot, p, i, f] for f in range(3)]
            own = level(z)
            lam, mu = L[p, pl.ds(8 * z, 8), :], M[p, pl.ds(8 * z, 8), :]
            sign = jnp.where(z_there[i], (-1.0, 1.0)[i], 0.0)
            slope = [sign * v for v in near]
            spread = lam * slope[2]
            S[p, 0, own, :] -= spread
            S[p, 1, own, :] -= spread
            S[p, 2, own, :] -= spread + (mu + mu) * slope[2]
            S[p, 4, own, :] -= mu * slope[0]
            S[p, 5, own, :] -= mu * slope[1]

        for i in range(2):
            @functools.partial(reach, i)
            def _(i=i):
                arrived(XR.at[slot, p, i, 0:3] if last else XR.at[slot, p, i], x_recv.at[slot, p, i])
                if not last:
                    arrived(ER.at[slot, p, i], e_recv.at[slot, p, i])

        for i, x, sign in ((0, 0, -1.0), (1, 7, 1.0)):
            near = [XR[slot, p, i, f] for f in range(3)]
            lam, mu = L[p, pl.ds(x, 8, stride=8), :], M[p, pl.ds(x, 8, stride=8), :]
            slope = [sign * v for v in near]
            spread = lam * slope[0]
            S[p, 0, column(x), :] -= spread + (mu + mu) * slope[0]
            S[p, 1, column(x), :] -= spread
            S[p, 2, column(x), :] -= spread
            S[p, 3, column(x), :] -= mu * slope[1]
            S[p, 4, column(x), :] -= mu * slope[2]

        if last:
            return
        for i, x, sign in ((0, 0, -1.0), (1, 7, 1.0)):
            near, far = [XR[slot, p, i, f] for f in range(3)], [XR[slot, p, i, 3 + f] for f in range(3)]
            lam, mu = LX[i, p], MX[i, p]
            dxs = [sign * (far[f] - V[p, f, column(x), :]) for f in range(3)]
            dzs = {}
            for k, f in enumerate((0, 2)):
                top, bottom = (jnp.where(z_there[j], ER[slot, p, i, j, k : k + 1, :], 0.0) for j in range(2))
                down = jnp.where(sub == 0, top, pltpu.roll(near[f], 1, 0))
                up = jnp.where(sub == 7, bottom, pltpu.roll(near[f], 7, 0))
                dzs[f] = up - down
            trace = dxs[0] + dy(near[1]) + dzs[2]
            beyond = column((-1, 8)[i])
            S[p, 0, beyond, :] -= lam * trace + (mu + mu) * dxs[0]
            S[p, 3, beyond, :] -= mu * (dy(near[0]) + dxs[1])
            S[p, 4, beyond, :] -= mu * (dzs[0] + dxs[2])
        for i, z, sign in ((0, 0, -1.0), (1, 7, 1.0)):
            near, far = [ZR[slot, p, i, f] for f in range(3)], [ZR[slot, p, i, 3 + f] for f in range(3)]
            lam, mu = LZ[i, p], MZ[i, p]
            dzs = [sign * (far[f] - V[p, f, level(z), :]) for f in range(3)]
            dxs = {}
            for k, f in enumerate((0, 2)):
                low, high = (ER[slot, p, j, i, k : k + 1, :] for j in range(2))
                behind = jnp.where(sub == 0, low, pltpu.roll(near[f], 1, 0))
                ahead = jnp.where(sub == 7, high, pltpu.roll(near[f], 7, 0))
                dxs[f] = ahead - behind
            trace = dxs[0] + dy(near[1]) + dzs[2]
            beyond = level((-1, 8)[i])
            S[p, 2, beyond, :] -= lam * trace + (mu + mu) * dzs[2]
            S[p, 4, beyond, :] -= mu * (dzs[0] + dxs[2])
            S[p, 5, beyond, :] -= mu * (dzs[1] + dy(near[2]))

    def each_part(then):
        def body(p, carry):
            then(p)
            return carry

        lax.fori_loop(0, 3, body, 0)

    move(MIDDLE, 0, 0, begin=True)

    arrived(YR, y_recv.at[0])
    low, high = YR[0, 8], YR[1, 8]
    seafloor = margin(low, high, STEPS).astype(jnp.int32)
    first_source = None
    for s in range(STEPS):
        v = jnp.where(dom == 0, margin(low, high, s), 0.0)
        first_source = v if s == 0 else first_source
        put_margin(SRC, (pl.ds(8 * s, 8), everywhere), v)
    for z in range(8):
        low, high = YR[0, z], YR[1, z]
        lam, mu, b, solid = materials(margin(low, high, 9).astype(jnp.int32), seafloor, z)
        for ref, v in ((L, lam), (M, mu), (B, b)):
            put_margin(ref, (pl.ds(8 * z, 8), everywhere), jnp.where(inside, v, 0.0))
        for f in range(9):
            v = margin(low, high, f)
            if f < 3:
                put_margin(V, (f, level(z), everywhere), v)
            else:
                if f >= 6:
                    v = jnp.where(solid, v, 0.0)
                elif z == 0:
                    v = v + first_source
                put_margin(S, (f - 3, level(z), everywhere), v)

    border((LEFT, RIGHT))

    def begin(p, carry):
        move(p, 0, 0, begin=True)
        return carry

    lax.fori_loop(1, 3, begin, 0)

    arrived(ZR0.at[:, 8:12], z_first_recv.at[1])
    for i in range(2):
        @functools.partial(reach, i)
        def _(i=i):
            arrived(XR0.at[i, 8:14], x_first_recv.at[1, i])
    for i in range(2):
        for k, ref in enumerate((LX, MX, SX)):
            tiles = three(XR0[i, 8 + 2 * k], XR0[i, 9 + 2 * k], margin(XR0[i, 6], XR0[i, 7], 3 + k))
            for p in range(3):
                ref[i, p] = tiles[p]
        for k, ref in enumerate((LZ, MZ)):
            tiles = three(ZR0[i, 8 + 2 * k], ZR0[i, 9 + 2 * k], margin(ZR0[i, 6], ZR0[i, 7], 3 + k))
            for p in range(3):
                ref[i, p] = jnp.where(z_there[i], tiles[p], 0.0)

    def step(s, carry):
        slot = lax.rem(s, 2)

        def turn(p):
            finish(p, 1 - slot)
            move(p, s, slot)

        each_part(turn)
        return carry

    lax.fori_loop(1, STEPS - 1, step, 0)

    end = STEPS - 1

    def final(p):
        finish(p, (end - 1) % 2)
        move(p, end, end % 2, last=True)

    each_part(final)

    def gather(f, ref, k):
        for z in range(8):
            middle, first_tile, second_tile = (ref[p, k, level(z), :] for p in (MIDDLE, LEFT, RIGHT))
            out[f, z, :, cut(0)] = jnp.where(lane < FIRST_CUT, first_tile, middle)
            out[f, z, :, cut(1)] = jnp.where(lane < SECOND_CUT, middle, second_tile)

    for f in range(3):
        gather(f, V, f)
    each_part(lambda p: finish(p, end % 2, last=True))
    for f in range(6):
        gather(3 + f, S, f)

    for i in range(2):
        arrived(OZ.at[i], z_send.at[i])

        @functools.partial(reach, i)
        def _(i=i):
            arrived(OX.at[i], x_send.at[i])
            arrived(OE.at[i], e_send.at[i])


def solution(mesh):
    sizes = (mesh.shape["dom"], mesh.shape["gx"], mesh.shape["gy"])

    def on_device(state, source, floor, region, lame, shear, buoy):
        hbm = pl.BlockSpec(memory_space=pltpu.HBM)

        def tiles(*shape):
            return pltpu.VMEM(shape + (8, 128), f32)

        return pl.pallas_call(
            functools.partial(kernel, sizes),
            out_shape=jax.ShapeDtypeStruct(state.shape, f32),
            in_specs=[hbm] * 7,
            out_specs=pl.BlockSpec(memory_space=pltpu.VMEM),
            scratch_shapes=[
                pltpu.VMEM(state.shape, f32),
                pltpu.VMEM(source.shape, f32),
                pltpu.VMEM(floor.shape, jnp.int32),
                pltpu.VMEM(region.shape, jnp.int32),
                pltpu.SMEM(lame.shape, f32),
                pltpu.SMEM(shear.shape, f32),
                pltpu.SMEM(buoy.shape, f32),
                pltpu.VMEM((3, 6, 10 * BLOCK, 128), f32),
                pltpu.VMEM((3, 3, 10 * BLOCK, 128), f32),
                pltpu.VMEM((3, 64, 128), f32),
                pltpu.VMEM((3, 64, 128), f32),
                pltpu.VMEM((3, 64, 128), f32),
                pltpu.VMEM((3, 8 * STEPS, 128), f32),
                tiles(2, 3),
                tiles(2, 3),
                tiles(2, 3),
                tiles(2, 3),
                tiles(2, 3),
                tiles(2, 113),
                tiles(2, 120),
                pltpu.VMEM((2, 3 * STEPS - 3, 2, 2, 128), f32),
                tiles(2, 14),
                tiles(2, 12),
                tiles(2, 9),
                tiles(2, 3, 2, 6),
                tiles(2, 3, 2, 6),
                pltpu.VMEM((2, 3, 2, 2, 2, 128), f32),
                pltpu.SemaphoreType.DMA((7,)),
                pltpu.SemaphoreType.DMA((2,)),
                pltpu.SemaphoreType.DMA((2,)),
                pltpu.SemaphoreType.DMA((2,)),
                pltpu.SemaphoreType.DMA((2, 2)),
                pltpu.SemaphoreType.DMA((2,)),
                pltpu.SemaphoreType.DMA((1,)),
                pltpu.SemaphoreType.DMA((2, 3, 2)),
                pltpu.SemaphoreType.DMA((2, 3)),
                pltpu.SemaphoreType.DMA((2, 3, 2)),
            ],
            compiler_params=pltpu.CompilerParams(
                collective_id=0, has_side_effects=True, vmem_limit_bytes=32 * 1024 * 1024
            ),
        )(*(
            pltpu.with_memory_space_constraint(v, pltpu.HBM)
            for v in (state, source, floor, region, lame, shear, buoy)
        ))

    return jax.shard_map(
        on_device,
        mesh=mesh,
        in_specs=(
            P(None, "dom", "gx", "gy"),
            P(None, "gx", "gy"),
            P("gx", "gy"),
            P("dom", "gx", "gy"),
            P(),
            P(),
            P(),
        ),
        out_specs=P(None, "dom", "gx", "gy"),
        check_vma=False,
    )
```

profile of v0, /device:TPU:96, one launch (start us, length us, event | category | flops | bytes accessed | tf_op | source)
XLA Modules:
  0.0 44.7 jit_solution(14114647896862461538)
XLA Ops:
  0.0 43.9 %shard_map.73 = f32[9,8,8,256]{3,2,1,0:T(8,128)S(1)} custom-call(f32[9,8,8,256]{3,2,1,0:T(8,128)} %state_in.1, f32[6,8,256]{2,1,0:T(8,128)} %source_in.1, s32[8,256]{1,0:T(8,128)} %floor_in.1, s32[8,8,256]{2,1,0:T(8,128)} %region_in.1, f32[16]{0:T(128)} %lame_in.1, f32[16]{0:T(128)} %shear_in.1, f32[16]{0:T(128)} %buoy_in.1), custom_call_target="tpu_custom_call" | custom-call | tf_op jit(solution)/shard_map/pallas_call | solution.py:545
  43.9 0.8 %copy.9 = f32[9,8,8,256]{3,2,1,0:T(8,128)} copy(f32[9,8,8,256]{3,2,1,0:T(8,128)S(1)} %shard_map.73) | data formatting | bytes 1179648
where the time goes:
time: 45.2 us; the launch traced here: 44.7 us
  Pallas kernels  43.9 us (97%)
  local copies, waits for them, and re-layouts  0.82 us (2%)
    pallas_call x1, Pallas kernels, on_device(): pl.pallas_call(functools.partial(kernel, sizes), out_shape=jax.ShapeDtype...  43.9 us

commit v1 on v0

v1 whole, which is shorter than its diff:
```python
import functools

import jax
import jax.numpy as jnp
from jax import lax
from jax.experimental import pallas as pl
from jax.experimental.pallas import tpu as pltpu
from jax.sharding import PartitionSpec as P

STEPS = 6
COURANT = 0.25
REGIONS = 16
BLOCK = 16
WIDE = 12
NEAR = 10
LEFT, RIGHT = 0, 1
PARTS = 2
MESH = pl.DeviceIdType.MESH

f32 = jnp.float32


def rows(z, x=0):
    return (z + 1) * BLOCK + 8 + x


def level(z):
    return pl.ds(rows(z), 8)


def column(x):
    return pl.ds(rows(0, x), 8, stride=BLOCK)


def dy(v):
    lane = lax.broadcasted_iota(jnp.int32, (8, 128), 1)
    ahead, behind = pltpu.roll(v, 127, 2), pltpu.roll(v, 1, 2)
    ahead = jnp.where(lane == 127, jnp.concatenate([ahead[1:], ahead[:1]], 0), ahead)
    behind = jnp.where(lane == 0, jnp.concatenate([behind[1:], behind[:1]], 0), behind)
    return ahead - behind


def pick(bits, table):
    values = list(table)
    for bit in bits:
        values = [jnp.where(bit, values[2 * i + 1], values[2 * i]) for i in range(len(values) // 2)]
    return values[0]


def kernel(
    sizes, state_in, source_in, floor_in, region_in, lame_in, shear_in, buoy_in, out,
    state, source, floor, region, lame, shear, buoy,
    S, V, L, M, B, SRC, LX, MX, SX, LZ, MZ, OX, OZ, OE, XR0, ZR0, YR, XR, ZR, ER,
    in_sem, x_send, z_send, e_send, x_first_recv, z_first_recv, y_recv, x_recv, z_recv, e_recv,
):
    n_dom, n_gx, n_gy = sizes
    dom, gx, gy = lax.axis_index("dom"), lax.axis_index("gx"), lax.axis_index("gy")
    lane = lax.broadcasted_iota(jnp.int32, (8, 128), 1)
    sub = lax.broadcasted_iota(jnp.int32, (8, 128), 0)
    zero = jnp.zeros((8, 128), f32)

    loads = [
        pltpu.make_async_copy(src, dst, in_sem.at[i])
        for i, (src, dst) in enumerate((
            (region_in, region), (floor_in, floor), (source_in, source), (state_in, state),
            (lame_in, lame), (shear_in, shear), (buoy_in, buoy)))
    ]
    for load in loads:
        load.start()

    sides = (-1, 1)
    there = [gx > 0, gx < n_gx - 1]
    z_there = [dom > 0, dom < n_dom - 1]

    doms = [dom, jnp.where(dom == n_dom - 1, 0, dom + 1), jnp.where(dom == 0, n_dom - 1, dom - 1)]
    gxs = [gx, gx + 1, gx - 1]
    gys = [gy, jnp.where(gy == n_gy - 1, 0, gy + 1), jnp.where(gy == 0, n_gy - 1, gy - 1)]

    def at(dz, dx, dyy):
        return (doms[dz], gxs[dx], gys[dyy])

    def reach(i, then):
        pl.when(there[i])(then)

    barrier = pltpu.get_barrier_semaphore()

    def greet(*way):
        pl.semaphore_signal(barrier, inc=1, device_id=at(*way), device_id_type=MESH)

    for i, dx in enumerate(sides):
        @functools.partial(reach, i)
        def _(dx=dx):
            for way in ((0, dx, 0), (-1, dx, 0), (1, dx, 0), (0, dx, -1), (0, dx, 1)):
                greet(*way)
    for way in [(a, 0, b) for a in (-1, 0, 1) for b in (-1, 0, 1) if a or b]:
        greet(*way)

    for i in range(2):
        @pl.when(jnp.logical_not(there[i]))
        def _(i=i):
            XR0[i] = jnp.zeros(XR0.shape[1:], f32)
            for slot in range(2):
                for p in range(PARTS):
                    XR[slot, p, i] = jnp.zeros(XR.shape[3:], f32)
                    ER[slot, p, i] = jnp.zeros(ER.shape[3:], f32)

    for p in range(PARTS):
        for f in range(3):
            for t in range(2):
                for z in range(-1, 9):
                    V[p, f, t, pl.ds(rows(z, -8), 8), :] = zero
                for z in (-1, 8):
                    V[p, f, t, level(z), :] = zero

    for load in loads[:4]:
        load.wait()

    def side_by_side(parts, t):
        tile = zero
        for k, v in enumerate(parts):
            shift = (WIDE * k + (WIDE if t else 0)) % 128
            v = pltpu.roll(v, shift, 1) if shift else v
            tile = jnp.where((lane >= WIDE * k) & (lane < WIDE * (k + 1)), v, tile)
        return tile

    def cut(t):
        return slice(128 * t, 128 * t + 128)

    for i in range(2):
        for z in range(8):
            OZ[i, 90 + z] = side_by_side(
                [state[f, z, :, cut(i)] for f in range(9)] + [region[z, :, cut(i)].astype(f32)], i)
        OZ[i, 98] = side_by_side([source[s, :, cut(i)] for s in range(STEPS)] + [floor[:, cut(i)].astype(f32)], i)

    def remote(src, dst, send, recv, way):
        return pltpu.make_async_remote_copy(
            src_ref=src, dst_ref=dst, send_sem=send, recv_sem=recv, device_id=at(*way), device_id_type=MESH)

    def xa_first(i):
        return remote(OX.at[i, 0:6], XR0.at[1 - i, 0:6], x_send.at[i], x_first_recv.at[0, 1 - i], (0, sides[i], 0))

    def xy_first(i, j):
        return remote(
            OX.at[i, 6 + j], XR0.at[1 - i, 7 - j], x_send.at[i], x_first_recv.at[0, 1 - i], (0, sides[i], sides[j]))

    def xb_first(i):
        return remote(OX.at[i, 8:14], XR0.at[1 - i, 8:14], x_send.at[i], x_first_recv.at[1, 1 - i], (0, sides[i], 0))

    def za_first(i):
        return remote(OZ.at[i, 0:6], ZR0.at[1 - i, 0:6], z_send.at[i], z_first_recv.at[0], (sides[i], 0, 0))

    def zy_first(i, j):
        return remote(
            OZ.at[i, 6 + j], ZR0.at[1 - i, 7 - j], z_send.at[i], z_first_recv.at[0], (sides[i], 0, sides[j]))

    def zb_first(i):
        return remote(OZ.at[i, 8:12], ZR0.at[1 - i, 8:12], z_send.at[i], z_first_recv.at[1], (sides[i], 0, 0))

    def y_first(i):
        return remote(OZ.at[i, 90:99], YR.at[1 - i], z_send.at[i], y_recv.at[0], (0, 0, sides[i]))

    def arrived(ref, sem):
        pltpu.make_async_copy(ref, ref, sem).wait()

    for load in loads[4:]:
        load.wait()
    scale = 0.5 * COURANT
    tables = [[t[k] * scale for k in range(REGIONS)] for t in (lame, shear, buoy)]

    def materials(number, seafloor, z):
        bits = [(number & (1 << k)) != 0 for k in range(4)]
        solid = (dom * 8 + z) >= seafloor
        lam, mu, b = (pick(bits, t) for t in tables)
        return lam, jnp.where(solid, mu, 0.0), b, solid

    def put(ref, index, pair):
        at_f, at_rows = index
        ref[(LEFT, *at_f, 0, at_rows)] = pair[0]
        ref[(RIGHT, *at_f, 0, at_rows)] = pair[1]
        ref[(LEFT, *at_f, 1, at_rows)] = jnp.where(lane < WIDE, pair[1], 0.0)
        ref[(RIGHT, *at_f, 1, at_rows)] = jnp.where(lane >= 128 - WIDE, pair[0], 0.0)

    def put_margin(ref, index, v):
        at_f, at_rows = index
        ref[(LEFT, *at_f, 1, at_rows)] = jnp.where(lane >= 128 - WIDE, v, ref[(LEFT, *at_f, 1, at_rows)])
        ref[(RIGHT, *at_f, 1, at_rows)] = jnp.where(lane < WIDE, v, ref[(RIGHT, *at_f, 1, at_rows)])

    for s in range(STEPS):
        put(SRC, ((), pl.ds(8 * s, 8)),
            [jnp.where(dom == 0, source[s, :, cut(t)], 0.0) for t in range(2)])
    for z in range(8):
        made = [materials(region[z, :, cut(t)], floor[:, cut(t)], z) for t in range(2)]
        for k, ref in enumerate((L, M, B)):
            put(ref, ((), pl.ds(8 * z, 8)), [m[k] for m in made])
        for f in range(9):
            v = [state[f, z, :, cut(t)] for t in range(2)]
            if f < 3:
                put(V, ((f,), level(z)), v)
            else:
                if f >= 6:
                    v = [jnp.where(m[3], w, 0.0) for m, w in zip(made, v)]
                elif z == 0:
                    v = [w + jnp.where(dom == 0, source[0, :, cut(t)], 0.0) for t, w in enumerate(v)]
                put(S, ((f - 3,), level(z)), v)

    x_fields, z_fields = (0, 3, 4), (2, 4, 5)
    pair = (LEFT, RIGHT)
    for i, x in ((0, 0), (1, 7)):
        parts = [[S[p, f, 0, column(x), :] for p in pair] for f in x_fields]
        parts += [[m[p, 0, pl.ds(x, 8, stride=8), :] for p in pair] for m in (L, M)]
        parts += [[
            jnp.concatenate([SRC[p, 0, pl.ds(x, STEPS, stride=8), :], jnp.zeros((8 - STEPS, 128), f32)], 0) for p in pair]]
        for k in range(6):
            for t in range(2):
                OX[i, 2 * k + t + (0 if k < 3 else 2)] = parts[k][t]
        for j in range(2):
            OX[i, 6 + j] = side_by_side([v[j] for v in parts], j)
    for i, z in ((0, 0), (1, 7)):
        parts = [[S[p, f, 0, level(z), :] for p in pair] for f in z_fields]
        parts += [[m[p, 0, pl.ds(8 * z, 8), :] for p in pair] for m in (L, M)]
        for k in range(5):
            for t in range(2):
                OZ[i, 2 * k + t + (0 if k < 3 else 2)] = parts[k][t]
        for j in range(2):
            OZ[i, 6 + j] = side_by_side([v[j] for v in parts], j)

    pl.semaphore_wait(barrier, 8 + 5 * (there[0].astype(jnp.int32) + there[1].astype(jnp.int32)))
    for i in range(2):
        @functools.partial(reach, i)
        def _(i=i):
            xa_first(i).start()
            for j in range(2):
                xy_first(i, j).start()
    for i in range(2):
        y_first(i).start()
        za_first(i).start()
        for j in range(2):
            zy_first(i, j).start()
    for i in range(2):
        @functools.partial(reach, i)
        def _(i=i):
            xb_first(i).start()
        zb_first(i).start()

    left = (lane >= 128 - WIDE) & (gy > 0)
    right = (lane < WIDE) & (gy < n_gy - 1)
    inside = left | right

    def margin(low, high, f):
        shift_r = (128 - WIDE * f) % 128
        shift_l = (256 - WIDE - WIDE * f) % 128
        a = pltpu.roll(high, shift_r, 1) if shift_r else high
        c = pltpu.roll(low, shift_l, 1) if shift_l else low
        return jnp.where(left, c, jnp.where(right, a, 0.0))

    def both(first_tile, second_tile, edge):
        return (
            jnp.stack([first_tile, jnp.where(lane < WIDE, second_tile, edge)]),
            jnp.stack([second_tile, jnp.where(lane >= 128 - WIDE, first_tile, edge)]),
        )

    def border():
        for i, x in ((0, -1), (1, 8)):
            for k, f in enumerate(x_fields):
                tiles = both(XR0[i, 2 * k], XR0[i, 2 * k + 1], margin(XR0[i, 6], XR0[i, 7], k))
                for p in range(PARTS):
                    S[p, f, :, column(x), :] = tiles[p]
        for i, z in ((0, -1), (1, 8)):
            for k, f in enumerate(z_fields):
                tiles = both(ZR0[i, 2 * k], ZR0[i, 2 * k + 1], margin(ZR0[i, 6], ZR0[i, 7], k))
                for p in range(PARTS):
                    S[p, f, :, level(z), :] = jnp.where(z_there[i], tiles[p], 0.0)

    def pack(tiles):
        out = zero
        for k, tile in enumerate(tiles):
            moved = pltpu.roll(tile, 2 * NEAR * k + NEAR, 1)
            out = jnp.where((lane >= 2 * NEAR * k) & (lane < 2 * NEAR * (k + 1)), moved, out)
        return out

    def fill(buffer, base, near, far):
        for f in range(3):
            buffer[base + f] = near[f][0]
            if far:
                buffer[base + 4 + f] = far[f][0]
        buffer[base + 3] = pack([v[1] for v in near + far])

    def opened(buffer, k):
        packed = pltpu.roll(buffer[3], (128 - 2 * NEAR * k - NEAR) % 128, 1)
        return jnp.stack([buffer[k if k < 3 else k + 1], packed])

    def x_base(p, s, last):
        return 14 + 14 * s + (4 * p if last else 7 * p)

    def z_base(p, s, last):
        return 12 + 14 * s + (4 * p if last else 7 * p)

    def x_copy(p, i, s, slot, last):
        n = 4 if last else 7
        return remote(
            OX.at[i, pl.ds(x_base(p, s, last), n)], XR.at[slot, p, 1 - i, 0:n], x_send.at[i], x_recv.at[slot, p, 1 - i],
            (0, sides[i], 0))

    def e_copy(p, i, j, s, slot):
        return remote(
            OE.at[i, 2 * s + p, j], ER.at[slot, p, 1 - i, 1 - j], e_send.at[i],
            e_recv.at[slot, p, 1 - i], (sides[j], sides[i], 0))

    def z_copy(p, i, s, slot, last):
        n = 4 if last else 7
        return remote(
            OZ.at[i, pl.ds(z_base(p, s, last), n)], ZR.at[slot, p, 1 - i, 0:n], z_send.at[i], z_recv.at[slot, p],
            (sides[i], 0, 0))

    def move(p, s, slot, begin=False, last=False):
        if not begin:
            at_step = pl.ds(8 * s if last else pl.multiple_of(8 * s, 8), 8)
            added = SRC[p, :, at_step, :]
            for f in range(3):
                S[p, f, :, level(0), :] += added
            for i, x in ((0, -1), (1, 8)):
                S[p, 0, :, pl.ds(rows(0, x), 1), :] += SX[i, p, :, pl.ds(s, 1), :]

        def accelerate(z):
            own = level(z)
            after, before = pl.ds(rows(z, 1), 8), pl.ds(rows(z, -1), 8)
            above, below = level(z + 1), level(z - 1)

            def dx(f):
                return S[p, f, :, after, :] - S[p, f, :, before, :]

            def dz(f):
                return S[p, f, :, above, :] - S[p, f, :, below, :]

            b = B[p, :, pl.ds(8 * z, 8), :]
            V[p, 0, :, own, :] -= b * (dx(0) + dy(S[p, 3, :, own, :]) + dz(4))
            V[p, 1, :, own, :] -= b * (dx(3) + dy(S[p, 1, :, own, :]) + dz(5))
            V[p, 2, :, own, :] -= b * (dx(4) + dy(S[p, 5, :, own, :]) + dz(2))

        for z in (0, 7):
            accelerate(z)
        if not last:
            for i, x in ((0, 0), (1, 7)):
                for j in range(2):
                    for k, f in enumerate((0, 2)):
                        for t in range(2):
                            OE[i, 2 * s + p, j, pl.ds(2 * k + t, 1), :] = V[p, f, t, pl.ds(rows(7 * j, x), 1), :]

                @functools.partial(reach, i)
                def _(i=i):
                    for j in range(2):
                        e_copy(p, i, j, s, slot).start()
        for z in range(1, 7):
            accelerate(z)
        base = x_base(p, s, last)
        for i, (x, inner) in enumerate(((0, 1), (7, 6))):
            fill(OX.at[i], base, [V[p, f, :, column(x), :] for f in range(3)],
                 [] if last else [V[p, f, :, column(inner), :] for f in range(3)])

            @functools.partial(reach, i)
            def _(i=i):
                x_copy(p, i, s, slot, last).start()
        base = z_base(p, s, last)
        for i, (z, inner) in enumerate(((0, 1), (7, 6))):
            fill(OZ.at[i], base, [V[p, f, :, level(z), :] for f in range(3)],
                 [] if last else [V[p, f, :, level(inner), :] for f in range(3)])
            z_copy(p, i, s, slot, last).start()

        for z in range(8):
            own = level(z)
            after, before = pl.ds(rows(z, 1), 8), pl.ds(rows(z, -1), 8)
            above, below = level(z + 1), level(z - 1)
            dxs = [V[p, f, :, after, :] - V[p, f, :, before, :] for f in range(3)]
            dzs = [V[p, f, :, above, :] - V[p, f, :, below, :] for f in range(3)]
            dys = [dy(V[p, f, :, own, :]) for f in range(3)]
            lam, mu = L[p, :, pl.ds(8 * z, 8), :], M[p, :, pl.ds(8 * z, 8), :]
            spread = lam * (dxs[0] + dys[1] + dzs[2])
            mu2 = mu + mu
            S[p, 0, :, own, :] -= spread + mu2 * dxs[0]
            S[p, 1, :, own, :] -= spread + mu2 * dys[1]
            S[p, 2, :, own, :] -= spread + mu2 * dzs[2]
            S[p, 3, :, own, :] -= mu * (dys[0] + dxs[1])
            S[p, 4, :, own, :] -= mu * (dzs[0] + dxs[2])
            S[p, 5, :, own, :] -= mu * (dzs[1] + dys[2])

    def edge_row(slot, p, i, j, k):
        return jnp.stack([ER[slot, p, i, j, pl.ds(2 * k + t, 1), :] for t in range(2)])

    def finish(p, slot, last=False):
        arrived(ZR.at[slot, p, :, 0:4] if last else ZR.at[slot, p], z_recv.at[slot, p])
        for i, z in ((0, 0), (1, 7)):
            near = [opened(ZR.at[slot, p, i], f) for f in range(3)]
            own = level(z)
            lam, mu = L[p, :, pl.ds(8 * z, 8), :], M[p, :, pl.ds(8 * z, 8), :]
            sign = jnp.where(z_there[i], (-1.0, 1.0)[i], 0.0)
            slope = [sign * v for v in near]
            spread = lam * slope[2]
            S[p, 0, :, own, :] -= spread
            S[p, 1, :, own, :] -= spread
            S[p, 2, :, own, :] -= spread + (mu + mu) * slope[2]
            S[p, 4, :, own, :] -= mu * slope[0]
            S[p, 5, :, own, :] -= mu * slope[1]

        for i in range(2):
            @functools.partial(reach, i)
            def _(i=i):
                arrived(XR.at[slot, p, i, 0:4] if last else XR.at[slot, p, i], x_recv.at[slot, p, i])
                if not last:
                    arrived(ER.at[slot, p, i], e_recv.at[slot, p, i])

        for i, x, sign in ((0, 0, -1.0), (1, 7, 1.0)):
            near = [opened(XR.at[slot, p, i], f) for f in range(3)]
            lam, mu = L[p, :, pl.ds(x, 8, stride=8), :], M[p, :, pl.ds(x, 8, stride=8), :]
            slope = [sign * v for v in near]
            spread = lam * slope[0]
            S[p, 0, :, column(x), :] -= spread + (mu + mu) * slope[0]
            S[p, 1, :, column(x), :] -= spread
            S[p, 2, :, column(x), :] -= spread
            S[p, 3, :, column(x), :] -= mu * slope[1]
            S[p, 4, :, column(x), :] -= mu * slope[2]

        if last:
            return
        for i, x, sign in ((0, 0, -1.0), (1, 7, 1.0)):
            got = [opened(XR.at[slot, p, i], k) for k in range(6)]
            near, far = got[:3], got[3:]
            lam, mu = LX[i, p], MX[i, p]
            dxs = [sign * (far[f] - V[p, f, :, column(x), :]) for f in range(3)]
            dzs = {}
            for k, f in enumerate((0, 2)):
                top, bottom = (jnp.where(z_there[j], edge_row(slot, p, i, j, k), 0.0) for j in range(2))
                down = jnp.where(sub == 0, top, pltpu.roll(near[f], 1, 1))
                up = jnp.where(sub == 7, bottom, pltpu.roll(near[f], 7, 1))
                dzs[f] = up - down
            trace = dxs[0] + dy(near[1]) + dzs[2]
            beyond = column((-1, 8)[i])
            S[p, 0, :, beyond, :] -= lam * trace + (mu + mu) * dxs[0]
            S[p, 3, :, beyond, :] -= mu * (dy(near[0]) + dxs[1])
            S[p, 4, :, beyond, :] -= mu * (dzs[0] + dxs[2])
        for i, z, sign in ((0, 0, -1.0), (1, 7, 1.0)):
            got = [opened(ZR.at[slot, p, i], k) for k in range(6)]
            near, far = got[:3], got[3:]
            lam, mu = LZ[i, p], MZ[i, p]
            dzs = [sign * (far[f] - V[p, f, :, level(z), :]) for f in range(3)]
            dxs = {}
            for k, f in enumerate((0, 2)):
                low, high = (edge_row(slot, p, j, i, k) for j in range(2))
                behind = jnp.where(sub == 0, low, pltpu.roll(near[f], 1, 1))
                ahead = jnp.where(sub == 7, high, pltpu.roll(near[f], 7, 1))
                dxs[f] = ahead - behind
            trace = dxs[0] + dy(near[1]) + dzs[2]
            beyond = level((-1, 8)[i])
            S[p, 2, :, beyond, :] -= lam * trace + (mu + mu) * dzs[2]
            S[p, 4, :, beyond, :] -= mu * (dzs[0] + dxs[2])
            S[p, 5, :, beyond, :] -= mu * (dzs[1] + dy(near[2]))

    def each_part(then):
        def body(p, carry):
            then(p)
            return carry

        lax.fori_loop(0, PARTS, body, 0)

    arrived(YR, y_recv.at[0])
    low, high = YR[0, 8], YR[1, 8]
    seafloor = margin(low, high, STEPS).astype(jnp.int32)
    first_source = None
    for s in range(STEPS):
        v = jnp.where(dom == 0, margin(low, high, s), 0.0)
        first_source = v if s == 0 else first_source
        put_margin(SRC, ((), pl.ds(8 * s, 8)), v)
    for z in range(8):
        low, high = YR[0, z], YR[1, z]
        lam, mu, b, solid = materials(margin(low, high, 9).astype(jnp.int32), seafloor, z)
        for ref, v in ((L, lam), (M, mu), (B, b)):
            put_margin(ref, ((), pl.ds(8 * z, 8)), jnp.where(inside, v, 0.0))
        for f in range(9):
            v = margin(low, high, f)
            if f < 3:
                put_margin(V, ((f,), level(z)), v)
            else:
                if f >= 6:
                    v = jnp.where(solid, v, 0.0)
                elif z == 0:
                    v = v + first_source
                put_margin(S, ((f - 3,), level(z)), v)

    arrived(ZR0.at[:, 0:8], z_first_recv.at[0])
    for i in range(2):
        @functools.partial(reach, i)
        def _(i=i):
            arrived(XR0.at[i, 0:8], x_first_recv.at[0, i])
    border()

    each_part(lambda p: move(p, 0, 0, begin=True))

    arrived(ZR0.at[:, 8:12], z_first_recv.at[1])
    for i in range(2):
        @functools.partial(reach, i)
        def _(i=i):
            arrived(XR0.at[i, 8:14], x_first_recv.at[1, i])
    for i in range(2):
        for k, ref in enumerate((LX, MX, SX)):
            tiles = both(XR0[i, 8 + 2 * k], XR0[i, 9 + 2 * k], margin(XR0[i, 6], XR0[i, 7], 3 + k))
            for p in range(PARTS):
                ref[i, p] = tiles[p]
        for k, ref in enumerate((LZ, MZ)):
            tiles = both(ZR0[i, 8 + 2 * k], ZR0[i, 9 + 2 * k], margin(ZR0[i, 6], ZR0[i, 7], 3 + k))
            for p in range(PARTS):
                ref[i, p] = jnp.where(z_there[i], tiles[p], 0.0)

    def step(s, carry):
        slot = lax.rem(s, 2)

        def turn(p):
            finish(p, 1 - slot)
            move(p, s, slot)

        each_part(turn)
        return carry

    lax.fori_loop(1, STEPS - 1, step, 0)

    end = STEPS - 1

    def final(p):
        finish(p, (end - 1) % 2)
        move(p, end, end % 2, last=True)

    each_part(final)

    def gather(f, ref, k):
        for z in range(8):
            for p in range(PARTS):
                out[f, z, :, cut(p)] = ref[p, k, 0, level(z), :]

    for f in range(3):
        gather(f, V, f)
    each_part(lambda p: finish(p, end % 2, last=True))
    for f in range(6):
        gather(3 + f, S, f)

    for i in range(2):
        arrived(OZ.at[i], z_send.at[i])

        @functools.partial(reach, i)
        def _(i=i):
            arrived(OX.at[i], x_send.at[i])
            arrived(OE.at[i], e_send.at[i])


def solution(mesh):
    sizes = (mesh.shape["dom"], mesh.shape["gx"], mesh.shape["gy"])

    def on_device(state, source, floor, region, lame, shear, buoy):
        hbm = pl.BlockSpec(memory_space=pltpu.HBM)

        def tiles(*shape):
            return pltpu.VMEM(shape + (8, 128), f32)

        return pl.pallas_call(
            functools.partial(kernel, sizes),
            out_shape=jax.ShapeDtypeStruct(state.shape, f32),
            in_specs=[hbm] * 7,
            out_specs=pl.BlockSpec(memory_space=pltpu.VMEM),
            scratch_shapes=[
                pltpu.VMEM(state.shape, f32),
                pltpu.VMEM(source.shape, f32),
                pltpu.VMEM(floor.shape, jnp.int32),
                pltpu.VMEM(region.shape, jnp.int32),
                pltpu.SMEM(lame.shape, f32),
                pltpu.SMEM(shear.shape, f32),
                pltpu.SMEM(buoy.shape, f32),
                pltpu.VMEM((PARTS, 6, 2, 10 * BLOCK, 128), f32),
                pltpu.VMEM((PARTS, 3, 2, 10 * BLOCK, 128), f32),
                pltpu.VMEM((PARTS, 2, 64, 128), f32),
                pltpu.VMEM((PARTS, 2, 64, 128), f32),
                pltpu.VMEM((PARTS, 2, 64, 128), f32),
                pltpu.VMEM((PARTS, 2, 8 * STEPS, 128), f32),
                tiles(2, PARTS, 2),
                tiles(2, PARTS, 2),
                tiles(2, PARTS, 2),
                tiles(2, PARTS, 2),
                tiles(2, PARTS, 2),
                tiles(2, 92),
                tiles(2, 99),
                pltpu.VMEM((2, PARTS * (STEPS - 1), 2, 4, 128), f32),
                tiles(2, 14),
                tiles(2, 12),
                tiles(2, 9),
                tiles(2, PARTS, 2, 7),
                tiles(2, PARTS, 2, 7),
                pltpu.VMEM((2, PARTS, 2, 2, 4, 128), f32),
                pltpu.SemaphoreType.DMA((7,)),
                pltpu.SemaphoreType.DMA((2,)),
                pltpu.SemaphoreType.DMA((2,)),
                pltpu.SemaphoreType.DMA((2,)),
                pltpu.SemaphoreType.DMA((2, 2)),
                pltpu.SemaphoreType.DMA((2,)),
                pltpu.SemaphoreType.DMA((1,)),
                pltpu.SemaphoreType.DMA((2, PARTS, 2)),
                pltpu.SemaphoreType.DMA((2, PARTS)),
                pltpu.SemaphoreType.DMA((2, PARTS, 2)),
            ],
            compiler_params=pltpu.CompilerParams(
                collective_id=0, has_side_effects=True, vmem_limit_bytes=32 * 1024 * 1024
            ),
        )(*(
            pltpu.with_memory_space_constraint(v, pltpu.HBM)
            for v in (state, source, floor, region, lame, shear, buoy)
        ))

    return jax.shard_map(
        on_device,
        mesh=mesh,
        in_specs=(
            P(None, "dom", "gx", "gy"),
            P(None, "gx", "gy"),
            P("gx", "gy"),
            P("dom", "gx", "gy"),
            P(),
            P(),
            P(),
        ),
        out_specs=P(None, "dom", "gx", "gy"),
        check_vma=False,
    )
```

time: 45.2 us -> 45.6 us (level)
  Pallas kernels: 43.9 us -> 44.7 us
    pallas_call x1, Pallas kernels: 43.9 us -> 44.7 us  [on_device(): pl.pallas_call(functools.partial(kernel, sizes), out_shape=jax.ShapeDtype...]
where the time goes in v1:
time: 45.6 us; the launch traced here: 45.5 us
  Pallas kernels  44.7 us (98%)
  local copies, waits for them, and re-layouts  0.82 us (2%)
    pallas_call x1, Pallas kernels, on_device(): pl.pallas_call(functools.partial(kernel, sizes), out_shape=jax.ShapeDtype...  44.7 us

profile of v1, /device:TPU:96, one launch (start us, length us, event | category | flops | bytes accessed | tf_op | source)
XLA Modules:
  0.0 45.5 jit_solution(1995280697987348978)
XLA Ops:
  0.0 44.7 %shard_map.73 = f32[9,8,8,256]{3,2,1,0:T(8,128)S(1)} custom-call(f32[9,8,8,256]{3,2,1,0:T(8,128)} %state_in.1, f32[6,8,256]{2,1,0:T(8,128)} %source_in.1, s32[8,256]{1,0:T(8,128)} %floor_in.1, s32[8,8,256]{2,1,0:T(8,128)} %region_in.1, f32[16]{0:T(128)} %lame_in.1, f32[16]{0:T(128)} %shear_in.1, f32[16]{0:T(128)} %buoy_in.1), custom_call_target="tpu_custom_call" | custom-call | tf_op jit(solution)/shard_map/pallas_call | solution.py:561
  44.7 0.8 %copy.9 = f32[9,8,8,256]{3,2,1,0:T(8,128)} copy(f32[9,8,8,256]{3,2,1,0:T(8,128)S(1)} %shard_map.73) | data formatting | bytes 1179648

commit v2 on v0

--- a/solution.py
+++ b/solution.py
@@ -120,41 +120,76 @@
     def cut(t):
         return slice(128 * t, 128 * t + 128)
 
+    def remote(src, dst, send, recv, way):
+        return pltpu.make_async_remote_copy(
+            src_ref=src, dst_ref=dst, send_sem=send, recv_sem=recv, device_id=at(*way), device_id_type=MESH)
+
+    def xa_first(i):
+        return remote(OX.at[i, 0:6], XR0.at[1 - i, 0:6], x_send.at[i], x_first_recv.at[0, 1 - i], (0, sides[i], 0))
+
+    def xy_first(i, j):
+        return remote(
+            OX.at[i, 6 + j], XR0.at[1 - i, 7 - j], x_send.at[i], x_first_recv.at[2, 1 - i], (0, sides[i], sides[j]))
+
+    def xb_first(i):
+        return remote(OX.at[i, 8:14], XR0.at[1 - i, 8:14], x_send.at[i], x_first_recv.at[1, 1 - i], (0, sides[i], 0))
+
+    def za_first(i):
+        return remote(OZ.at[i, 0:6], ZR0.at[1 - i, 0:6], z_send.at[i], z_first_recv.at[0], (sides[i], 0, 0))
+
+    def zy_first(i, j):
+        return remote(
+            OZ.at[i, 6 + j], ZR0.at[1 - i, 7 - j], z_send.at[i], z_first_recv.at[2], (sides[i], 0, sides[j]))
+
+    def zb_first(i):
+        return remote(OZ.at[i, 8:12], ZR0.at[1 - i, 8:12], z_send.at[i], z_first_recv.at[1], (sides[i], 0, 0))
+
+    def y_first(i):
+        return remote(OZ.at[i, 111:120], YR.at[1 - i], z_send.at[i], y_recv.at[0], (0, 0, sides[i]))
+
+    def arrived(ref, sem):
+        pltpu.make_async_copy(ref, ref, sem).wait()
+
+    def put(ref, index, pair):
+        ref[(MIDDLE, *index)] = jnp.where(lane < SEAM, pair[1], pair[0])
+        ref[(LEFT, *index)] = pair[0]
+        ref[(RIGHT, *index)] = pair[1]
+
+    def put_margin(ref, index, v):
+        ref[(LEFT, *index)] = jnp.where(lane >= 128 - WIDE, v, ref[(LEFT, *index)])
+        ref[(RIGHT, *index)] = jnp.where(lane < WIDE, v, ref[(RIGHT, *index)])
+
+    everywhere = slice(None)
+    for z in range(8):
+        solid = [(dom * 8 + z) >= floor[:, cut(t)] for t in range(2)]
+        for f in range(6):
+            v = [state[3 + f, z, :, cut(t)] for t in range(2)]
+            if f >= 3:
+                v = [jnp.where(m, w, 0.0) for m, w in zip(solid, v)]
+            elif z == 0:
+                v = [w + jnp.where(dom == 0, source[0, :, cut(t)], 0.0) for t, w in enumerate(v)]
+            put(S, (f, level(z), everywhere), v)
+    x_fields, z_fields = (0, 3, 4), (2, 4, 5)
+    pair = (LEFT, RIGHT)
+    for i, at_edge in enumerate((0, 7)):
+        for k in range(3):
+            for t in range(2):
+                OX[i, 2 * k + t] = S[pair[t], x_fields[k], column(at_edge), :]
+                OZ[i, 2 * k + t] = S[pair[t], z_fields[k], level(at_edge), :]
     for i in range(2):
         for z in range(8):
             OZ[i, 111 + z] = side_by_side(
                 [state[f, z, :, cut(i)] for f in range(9)] + [region[z, :, cut(i)].astype(f32)], i)
         OZ[i, 119] = side_by_side([source[s, :, cut(i)] for s in range(STEPS)] + [floor[:, cut(i)].astype(f32)], i)
 
-    def remote(src, dst, send, recv, way):
-        return pltpu.make_async_remote_copy(
-            src_ref=src, dst_ref=dst, send_sem=send, recv_sem=recv, device_id=at(*way), device_id_type=MESH)
-
-    def xa_first(i):
-        return remote(OX.at[i, 0:6], XR0.at[1 - i, 0:6], x_send.at[i], x_first_recv.at[0, 1 - i], (0, sides[i], 0))
-
-    def xy_first(i, j):
-        return remote(
-            OX.at[i, 6 + j], XR0.at[1 - i, 7 - j], x_send.at[i], x_first_recv.at[0, 1 - i], (0, sides[i], sides[j]))
-
-    def xb_first(i):
-        return remote(OX.at[i, 8:14], XR0.at[1 - i, 8:14], x_send.at[i], x_first_recv.at[1, 1 - i], (0, sides[i], 0))
-
-    def za_first(i):
-        return remote(OZ.at[i, 0:6], ZR0.at[1 - i, 0:6], z_send.at[i], z_first_recv.at[0], (sides[i], 0, 0))
-
-    def zy_first(i, j):
-        return remote(
-            OZ.at[i, 6 + j], ZR0.at[1 - i, 7 - j], z_send.at[i], z_first_recv.at[0], (sides[i], 0, sides[j]))
-
-    def zb_first(i):
-        return remote(OZ.at[i, 8:12], ZR0.at[1 - i, 8:12], z_send.at[i], z_first_recv.at[1], (sides[i], 0, 0))
-
-    def y_first(i):
-        return remote(OZ.at[i, 111:120], YR.at[1 - i], z_send.at[i], y_recv.at[0], (0, 0, sides[i]))
-
-    def arrived(ref, sem):
-        pltpu.make_async_copy(ref, ref, sem).wait()
+    pl.semaphore_wait(barrier, 8 + 5 * (there[0].astype(jnp.int32) + there[1].astype(jnp.int32)))
+    for i in range(2):
+        @functools.partial(reach, i)
+        def _(i=i):
+            xa_first(i).start()
+    for i in range(2):
+        za_first(i).start()
+        y_first(i).start()
 
     for load in loads[4:]:
         load.wait()
@@ -167,16 +202,6 @@
         lam, mu, b = (pick(bits, t) for t in tables)
         return lam, jnp.where(solid, mu, 0.0), b, solid
 
-    def put(ref, index, pair):
-        ref[(MIDDLE, *index)] = jnp.where(lane < SEAM, pair[1], pair[0])
-        ref[(LEFT, *index)] = pair[0]
-        ref[(RIGHT, *index)] = pair[1]
-
-    def put_margin(ref, index, v):
-        ref[(LEFT, *index)] = jnp.where(lane >= 128 - WIDE, v, ref[(LEFT, *index)])
-        ref[(RIGHT, *index)] = jnp.where(lane < WIDE, v, ref[(RIGHT, *index)])
-
-    everywhere = slice(None)
     for s in range(STEPS):
         put(SRC, (pl.ds(8 * s, 8), everywhere),
             [jnp.where(dom == 0, source[s, :, cut(t)], 0.0) for t in range(2)])
@@ -184,54 +209,34 @@
         made = [materials(region[z, :, cut(t)], floor[:, cut(t)], z) for t in range(2)]
         for k, ref in enumerate((L, M, B)):
             put(ref, (pl.ds(8 * z, 8), everywhere), [m[k] for m in made])
-        for f in range(9):
-            v = [state[f, z, :, cut(t)] for t in range(2)]
-            if f < 3:
-                put(V, (f, level(z), everywhere), v)
-            else:
-                if f >= 6:
-                    v = [jnp.where(m[3], w, 0.0) for m, w in zip(made, v)]
-                elif z == 0:
-                    v = [w + jnp.where(dom == 0, source[0, :, cut(t)], 0.0) for t, w in enumerate(v)]
-                put(S, (f - 3, level(z), everywhere), v)
-
-    x_fields, z_fields = (0, 3, 4), (2, 4, 5)
-    pair = (LEFT, RIGHT)
+        for f in range(3):
+            put(V, (f, level(z), everywhere), [state[f, z, :, cut(t)] for t in range(2)])
+
     for i, x in ((0, 0), (1, 7)):
-        parts = [[S[p, f, column(x), :] for p in pair] for f in x_fields]
+        parts = [[OX[i, 2 * k + t] for t in range(2)] for k in range(3)]
         parts += [[m[p, pl.ds(x, 8, stride=8), :] for p in pair] for m in (L, M)]
         parts += [[
             jnp.concatenate([SRC[p, pl.ds(x, STEPS, stride=8), :], jnp.zeros((8 - STEPS, 128), f32)], 0) for p in pair]]
-        for k in range(6):
+        for k in range(3, 6):
             for t in range(2):
-                OX[i, 2 * k + t + (0 if k < 3 else 2)] = parts[k][t]
+                OX[i, 2 * k + t + 2] = parts[k][t]
         for j in range(2):
             OX[i, 6 + j] = side_by_side([v[j] for v in parts], j)
+
+        @functools.partial(reach, i)
+        def _(i=i):
+            for j in range(2):
+                xy_first(i, j).start()
+            xb_first(i).start()
     for i, z in ((0, 0), (1, 7)):
-        parts = [[S[p, f, level(z), :] for p in pair] for f in z_fields]
+        parts = [[OZ[i, 2 * k + t] for t in range(2)] for k in range(3)]
         parts += [[m[p, pl.ds(8 * z, 8), :] for p in pair] for m in (L, M)]
-        for k in range(5):
+        for k in range(3, 5):
             for t in range(2):
-                OZ[i, 2 * k + t + (0 if k < 3 else 2)] = parts[k][t]
+                OZ[i, 2 * k + t + 2] = parts[k][t]
         for j in range(2):
             OZ[i, 6 + j] = side_by_side([v[j] for v in parts], j)
-
-    pl.semaphore_wait(barrier, 8 + 5 * (there[0].astype(jnp.int32) + there[1].astype(jnp.int32)))
-    for i in range(2):
-        @functools.partial(reach, i)
-        def _(i=i):
-            xa_first(i).start()
-            for j in range(2):
-                xy_first(i, j).start()
-    for i in range(2):
-        y_first(i).start()
-        za_first(i).start()
-        for j in range(2):
             zy_first(i, j).start()
-    for i in range(2):
-        @functools.partial(reach, i)
-        def _(i=i):
-            xb_first(i).start()
         zb_first(i).start()
 
     left = (lane >= 128 - WIDE) & (gy > 0)
@@ -245,11 +250,11 @@
         c = pltpu.roll(low, shift_l, 1) if shift_l else low
         return jnp.where(left, c, jnp.where(right, a, 0.0))
 
-    arrived(ZR0.at[:, 0:8], z_first_recv.at[0])
+    arrived(ZR0.at[:, 0:6], z_first_recv.at[0])
     for i in range(2):
         @functools.partial(reach, i)
         def _(i=i):
-            arrived(XR0.at[i, 0:8], x_first_recv.at[0, i])
+            arrived(XR0.at[i, 0:6], x_first_recv.at[0, i])
 
     def three(first_tile, second_tile, edge):
         return (
@@ -296,15 +301,7 @@
             OZ.at[i, pl.ds(z_base(p, s, last), n)], ZR.at[slot, p, 1 - i, 0:n], z_send.at[i], z_recv.at[slot, p],
             (sides[i], 0, 0))
 
-    def move(p, s, slot, begin=False, last=False):
-        if not begin:
-            at_step = pl.ds(8 * s if last else pl.multiple_of(8 * s, 8), 8)
-            added = SRC[p, at_step, :]
-            for f in range(3):
-                S[p, f, level(0), :] += added
-            for i, x in ((0, -1), (1, 8)):
-                S[p, 0, pl.ds(rows(0, x), 1), :] += SX[i, p, pl.ds(s, 1), :]
-
+    def move(p, s, slot, last=False):
         def accelerate(z):
             own = level(z)
             after, before = pl.ds(rows(z, 1), 8), pl.ds(rows(z, -1), 8)
@@ -370,7 +367,14 @@
             S[p, 4, own, :] -= mu * (dzs[0] + dxs[2])
             S[p, 5, own, :] -= mu * (dzs[1] + dys[2])
 
-    def finish(p, slot, last=False):
+    def finish(p, slot, then=None):
+        last = then is None
+        if not last:
+            added = SRC[p, pl.ds(8 * then if isinstance(then, int) else pl.multiple_of(8 * then, 8), 8), :]
+            for f in range(3):
+                S[p, f, level(0), :] += added
+            for i, x in ((0, -1), (1, 8)):
+                S[p, 0, pl.ds(rows(0, x), 1), :] += SX[i, p, pl.ds(then, 1), :]
         arrived(ZR.at[slot, p, :, 0:3] if last else ZR.at[slot, p], z_recv.at[slot, p])
         for i, z in ((0, 0), (1, 7)):
             near = [ZR[slot, p, i, f] for f in range(3)]
@@ -389,8 +393,6 @@
             @functools.partial(reach, i)
             def _(i=i):
                 arrived(XR.at[slot, p, i, 0:3] if last else XR.at[slot, p, i], x_recv.at[slot, p, i])
-                if not last:
-                    arrived(ER.at[slot, p, i], e_recv.at[slot, p, i])
 
         for i, x, sign in ((0, 0, -1.0), (1, 7, 1.0)):
             near = [XR[slot, p, i, f] for f in range(3)]
@@ -410,11 +412,9 @@
             lam, mu = LX[i, p], MX[i, p]
             dxs = [sign * (far[f] - V[p, f, column(x), :]) for f in range(3)]
             dzs = {}
-            for k, f in enumerate((0, 2)):
-                top, bottom = (jnp.where(z_there[j], ER[slot, p, i, j, k : k + 1, :], 0.0) for j in range(2))
-                down = jnp.where(sub == 0, top, pltpu.roll(near[f], 1, 0))
-                up = jnp.where(sub == 7, bottom, pltpu.roll(near[f], 7, 0))
-                dzs[f] = up - down
+            for f in (0, 2):
+                up, down = pltpu.roll(near[f], 7, 0), pltpu.roll(near[f], 1, 0)
+                dzs[f] = jnp.where(sub == 7, 0.0, up) - jnp.where(sub == 0, 0.0, down)
             trace = dxs[0] + dy(near[1]) + dzs[2]
             beyond = column((-1, 8)[i])
             S[p, 0, beyond, :] -= lam * trace + (mu + mu) * dxs[0]
@@ -425,17 +425,31 @@
             lam, mu = LZ[i, p], MZ[i, p]
             dzs = [sign * (far[f] - V[p, f, level(z), :]) for f in range(3)]
             dxs = {}
-            for k, f in enumerate((0, 2)):
-                low, high = (ER[slot, p, j, i, k : k + 1, :] for j in range(2))
-                behind = jnp.where(sub == 0, low, pltpu.roll(near[f], 1, 0))
-                ahead = jnp.where(sub == 7, high, pltpu.roll(near[f], 7, 0))
-                dxs[f] = ahead - behind
+            for f in (0, 2):
+                ahead, behind = pltpu.roll(near[f], 7, 0), pltpu.roll(near[f], 1, 0)
+                dxs[f] = jnp.where(sub == 7, 0.0, ahead) - jnp.where(sub == 0, 0.0, behind)
             trace = dxs[0] + dy(near[1]) + dzs[2]
             beyond = level((-1, 8)[i])
             S[p, 2, beyond, :] -= lam * trace + (mu + mu) * dzs[2]
             S[p, 4, beyond, :] -= mu * (dzs[0] + dxs[2])
             S[p, 5, beyond, :] -= mu * (dzs[1] + dy(near[2]))
 
+        for i in range(2):
+            @functools.partial(reach, i)
+            def _(i=i):
+                arrived(ER.at[slot, p, i], e_recv.at[slot, p, i])
+        for i, x in ((0, 0), (1, 7)):
+            for j, z in ((0, 0), (1, 7)):
+                edge_x, edge_z = (ER[slot, p, i, j, k : k + 1, :] for k in range(2))
+                sign = jnp.where(z_there[j], (-1.0, 1.0)[j], 0.0)
+                outer = pl.ds(rows(z, (-1, 8)[i]), 1)
+                at_z, at_x = slice(z, z + 1), slice(x, x + 1)
+                S[p, 0, outer, :] -= LX[i, p, at_z, :] * (sign * edge_z)
+                S[p, 4, outer, :] -= MX[i, p, at_z, :] * (sign * edge_x)
+                outer = pl.ds(rows((-1, 8)[j], x), 1)
+                S[p, 2, outer, :] -= LZ[j, p, at_x, :] * (sides[i] * edge_x)
+                S[p, 4, outer, :] -= MZ[j, p, at_x, :] * (sides[i] * edge_z)
+
     def each_part(then):
         def body(p, carry):
             then(p)
@@ -443,7 +457,7 @@
 
         lax.fori_loop(0, 3, body, 0)
 
-    move(MIDDLE, 0, 0, begin=True)
+    move(MIDDLE, 0, 0)
 
     arrived(YR, y_recv.at[0])
     low, high = YR[0, 8], YR[1, 8]
@@ -469,10 +483,15 @@
                     v = v + first_source
                 put_margin(S, (f - 3, level(z), everywhere), v)
 
+    arrived(ZR0.at[:, 6:8], z_first_recv.at[2])
+    for i in range(2):
+        @functools.partial(reach, i)
+        def _(i=i):
+            arrived(XR0.at[i, 6:8], x_first_recv.at[2, i])
     border((LEFT, RIGHT))
 
     def begin(p, carry):
-        move(p, 0, 0, begin=True)
+        move(p, 0, 0)
         return carry
 
     lax.fori_loop(1, 3, begin, 0)
@@ -496,7 +515,7 @@
         slot = lax.rem(s, 2)
 
         def turn(p):
-            finish(p, 1 - slot)
+            finish(p, 1 - slot, s)
             move(p, s, slot)
 
         each_part(turn)
@@ -507,7 +526,7 @@
     end = STEPS - 1
 
     def final(p):
-        finish(p, (end - 1) % 2)
+        finish(p, (end - 1) % 2, end)
         move(p, end, end % 2, last=True)
 
     each_part(final)
@@ -520,7 +539,7 @@
 
     for f in range(3):
         gather(f, V, f)
-    each_part(lambda p: finish(p, end % 2, last=True))
+    each_part(lambda p: finish(p, end % 2))
     for f in range(6):
         gather(3 + f, S, f)
 
@@ -579,8 +598,8 @@
                 pltpu.SemaphoreType.DMA((2,)),
                 pltpu.SemaphoreType.DMA((2,)),
                 pltpu.SemaphoreType.DMA((2,)),
-                pltpu.SemaphoreType.DMA((2, 2)),
-                pltpu.SemaphoreType.DMA((2,)),
+                pltpu.SemaphoreType.DMA((3, 2)),
+                pltpu.SemaphoreType.DMA((3,)),
                 pltpu.SemaphoreType.DMA((1,)),
                 pltpu.SemaphoreType.DMA((2, 3, 2)),
                 pltpu.SemaphoreType.DMA((2, 3)),

time: 45.2 us -> 44.9 us (level)
  no operation moved by 1% of the time
where the time goes in v2:
time: 44.9 us; the launch traced here: 44.8 us
  Pallas kernels  44 us (98%)
  local copies, waits for them, and re-layouts  0.82 us (2%)
    pallas_call x1, Pallas kernels, on_device(): pl.pallas_call(functools.partial(kernel, sizes), out_shape=jax.ShapeDtype...  44 us

profile of v2, /device:TPU:96, one launch (start us, length us, event | category | flops | bytes accessed | tf_op | source)
XLA Modules:
  0.0 44.8 jit_solution(13401955400043653110)
XLA Ops:
  0.0 44.0 %shard_map.73 = f32[9,8,8,256]{3,2,1,0:T(8,128)S(1)} custom-call(f32[9,8,8,256]{3,2,1,0:T(8,128)} %state_in.1, f32[6,8,256]{2,1,0:T(8,128)} %source_in.1, s32[8,256]{1,0:T(8,128)} %floor_in.1, s32[8,8,256]{2,1,0:T(8,128)} %region_in.1, f32[16]{0:T(128)} %lame_in.1, f32[16]{0:T(128)} %shear_in.1, f32[16]{0:T(128)} %buoy_in.1), custom_call_target="tpu_custom_call" | custom-call | tf_op jit(solution)/shard_map/pallas_call | solution.py:564
  44.0 0.8 %copy.9 = f32[9,8,8,256]{3,2,1,0:T(8,128)} copy(f32[9,8,8,256]{3,2,1,0:T(8,128)S(1)} %shard_map.73) | data formatting | bytes 1179648

commit v3 on v2

--- a/solution.py
+++ b/solution.py
@@ -302,24 +302,27 @@
             (sides[i], 0, 0))
 
     def move(p, s, slot, last=False):
-        def accelerate(z):
-            own = level(z)
-            after, before = pl.ds(rows(z, 1), 8), pl.ds(rows(z, -1), 8)
-            above, below = level(z + 1), level(z - 1)
-
-            def dx(f):
-                return S[p, f, after, :] - S[p, f, before, :]
-
-            def dz(f):
-                return S[p, f, above, :] - S[p, f, below, :]
-
-            b = B[p, pl.ds(8 * z, 8), :]
-            V[p, 0, own, :] -= b * (dx(0) + dy(S[p, 3, own, :]) + dz(4))
-            V[p, 1, own, :] -= b * (dx(3) + dy(S[p, 1, own, :]) + dz(5))
-            V[p, 2, own, :] -= b * (dx(4) + dy(S[p, 5, own, :]) + dz(2))
-
-        for z in (0, 7):
-            accelerate(z)
+        def accelerate(levels):
+            moved = []
+            for z in levels:
+                own = level(z)
+                after, before = pl.ds(rows(z, 1), 8), pl.ds(rows(z, -1), 8)
+                above, below = level(z + 1), level(z - 1)
+
+                def dx(f):
+                    return S[p, f, after, :] - S[p, f, before, :]
+
+                def dz(f):
+                    return S[p, f, above, :] - S[p, f, below, :]
+
+                b = B[p, pl.ds(8 * z, 8), :]
+                moved.append((0, own, V[p, 0, own, :] - b * (dx(0) + dy(S[p, 3, own, :]) + dz(4))))
+                moved.append((1, own, V[p, 1, own, :] - b * (dx(3) + dy(S[p, 1, own, :]) + dz(5))))
+                moved.append((2, own, V[p, 2, own, :] - b * (dx(4) + dy(S[p, 5, own, :]) + dz(2))))
+            for f, own, v in moved:
+                V[p, f, own, :] = v
+
+        accelerate((0, 7))
         if not last:
             for i, x in ((0, 0), (1, 7)):
                 for j in range(2):
@@ -330,14 +333,12 @@
                 def _(i=i):
                     for j in range(2):
                         e_copy(p, i, j, s, slot).start()
-        for z in range(1, 7):
-            accelerate(z)
+        accelerate((1, 2, 3))
+        accelerate((4, 5, 6))
         base = x_base(p, s, last)
         for i, (x, inner) in enumerate(((0, 1), (7, 6))):
-            for f in range(3):
-                OX[i, base + f] = V[p, f, column(x), :]
-                if not last:
-                    OX[i, base + 3 + f] = V[p, f, column(inner), :]
+            for k, v in enumerate([V[p, f, column(c), :] for c in ((x,) if last else (x, inner)) for f in range(3)]):
+                OX[i, base + k] = v
 
             @functools.partial(reach, i)
             def _(i=i):
@@ -350,6 +351,7 @@
                     OZ[i, base + 3 + f] = V[p, f, level(inner), :]
             z_copy(p, i, s, slot, last).start()
 
+        later = []
         for z in range(8):
             own = level(z)
             after, before = pl.ds(rows(z, 1), 8), pl.ds(rows(z, -1), 8)
@@ -360,22 +362,29 @@
             lam, mu = L[p, pl.ds(8 * z, 8), :], M[p, pl.ds(8 * z, 8), :]
             spread = lam * (dxs[0] + dys[1] + dzs[2])
             mu2 = mu + mu
-            S[p, 0, own, :] -= spread + mu2 * dxs[0]
-            S[p, 1, own, :] -= spread + mu2 * dys[1]
-            S[p, 2, own, :] -= spread + mu2 * dzs[2]
-            S[p, 3, own, :] -= mu * (dys[0] + dxs[1])
-            S[p, 4, own, :] -= mu * (dzs[0] + dxs[2])
-            S[p, 5, own, :] -= mu * (dzs[1] + dys[2])
+            change = (
+                spread + mu2 * dxs[0], spread + mu2 * dys[1], spread + mu2 * dzs[2],
+                mu * (dys[0] + dxs[1]), mu * (dzs[0] + dxs[2]), mu * (dzs[1] + dys[2]))
+            later += [(f, own, S[p, f, own, :] - change[f]) for f in range(6)]
+            if z % 2:
+                write(p, later)
+                later = []
+
+    def write(p, results):
+        for f, at_rows, v in results:
+            S[p, f, at_rows, :] = v
 
     def finish(p, slot, then=None):
         last = then is None
         if not last:
             added = SRC[p, pl.ds(8 * then if isinstance(then, int) else pl.multiple_of(8 * then, 8), 8), :]
-            for f in range(3):
-                S[p, f, level(0), :] += added
+            results = [(f, level(0), S[p, f, level(0), :] + added) for f in range(3)]
             for i, x in ((0, -1), (1, 8)):
-                S[p, 0, pl.ds(rows(0, x), 1), :] += SX[i, p, pl.ds(then, 1), :]
+                outer = pl.ds(rows(0, x), 1)
+                results.append((0, outer, S[p, 0, outer, :] + SX[i, p, pl.ds(then, 1), :]))
+            write(p, results)
         arrived(ZR.at[slot, p, :, 0:3] if last else ZR.at[slot, p], z_recv.at[slot, p])
+        results = []
         for i, z in ((0, 0), (1, 7)):
             near = [ZR[slot, p, i, f] for f in range(3)]
             own = level(z)
@@ -383,29 +392,32 @@
             sign = jnp.where(z_there[i], (-1.0, 1.0)[i], 0.0)
             slope = [sign * v for v in near]
             spread = lam * slope[2]
-            S[p, 0, own, :] -= spread
-            S[p, 1, own, :] -= spread
-            S[p, 2, own, :] -= spread + (mu + mu) * slope[2]
-            S[p, 4, own, :] -= mu * slope[0]
-            S[p, 5, own, :] -= mu * slope[1]
+            results.append((0, own, S[p, 0, own, :] - (spread)))
+            results.append((1, own, S[p, 1, own, :] - (spread)))
+            results.append((2, own, S[p, 2, own, :] - (spread + (mu + mu) * slope[2])))
+            results.append((4, own, S[p, 4, own, :] - (mu * slope[0])))
+            results.append((5, own, S[p, 5, own, :] - (mu * slope[1])))
+        write(p, results)
 
         for i in range(2):
             @functools.partial(reach, i)
             def _(i=i):
                 arrived(XR.at[slot, p, i, 0:3] if last else XR.at[slot, p, i], x_recv.at[slot, p, i])
 
+        results = []
         for i, x, sign in ((0, 0, -1.0), (1, 7, 1.0)):
             near = [XR[slot, p, i, f] for f in range(3)]
             lam, mu = L[p, pl.ds(x, 8, stride=8), :], M[p, pl.ds(x, 8, stride=8), :]
             slope = [sign * v for v in near]
             spread = lam * slope[0]
-            S[p, 0, column(x), :] -= spread + (mu + mu) * slope[0]
-            S[p, 1, column(x), :] -= spread
-            S[p, 2, column(x), :] -= spread
-            S[p, 3, column(x), :] -= mu * slope[1]
-            S[p, 4, column(x), :] -= mu * slope[2]
+            results.append((0, column(x), S[p, 0, column(x), :] - (spread + (mu + mu) * slope[0])))
+            results.append((1, column(x), S[p, 1, column(x), :] - (spread)))
+            results.append((2, column(x), S[p, 2, column(x), :] - (spread)))
+            results.append((3, column(x), S[p, 3, column(x), :] - (mu * slope[1])))
+            results.append((4, column(x), S[p, 4, column(x), :] - (mu * slope[2])))
 
         if last:
+            write(p, results)
             return
         for i, x, sign in ((0, 0, -1.0), (1, 7, 1.0)):
             near, far = [XR[slot, p, i, f] for f in range(3)], [XR[slot, p, i, 3 + f] for f in range(3)]
@@ -417,9 +429,9 @@
                 dzs[f] = jnp.where(sub == 7, 0.0, up) - jnp.where(sub == 0, 0.0, down)
             trace = dxs[0] + dy(near[1]) + dzs[2]
             beyond = column((-1, 8)[i])
-            S[p, 0, beyond, :] -= lam * trace + (mu + mu) * dxs[0]
-            S[p, 3, beyond, :] -= mu * (dy(near[0]) + dxs[1])
-            S[p, 4, beyond, :] -= mu * (dzs[0] + dxs[2])
+            results.append((0, beyond, S[p, 0, beyond, :] - (lam * trace + (mu + mu) * dxs[0])))
+            results.append((3, beyond, S[p, 3, beyond, :] - (mu * (dy(near[0]) + dxs[1]))))
+            results.append((4, beyond, S[p, 4, beyond, :] - (mu * (dzs[0] + dxs[2]))))
         for i, z, sign in ((0, 0, -1.0), (1, 7, 1.0)):
             near, far = [ZR[slot, p, i, f] for f in range(3)], [ZR[slot, p, i, 3 + f] for f in range(3)]
             lam, mu = LZ[i, p], MZ[i, p]
@@ -430,32 +442,33 @@
                 dxs[f] = jnp.where(sub == 7, 0.0, ahead) - jnp.where(sub == 0, 0.0, behind)
             trace = dxs[0] + dy(near[1]) + dzs[2]
             beyond = level((-1, 8)[i])
-            S[p, 2, beyond, :] -= lam * trace + (mu + mu) * dzs[2]
-            S[p, 4, beyond, :] -= mu * (dzs[0] + dxs[2])
-            S[p, 5, beyond, :] -= mu * (dzs[1] + dy(near[2]))
+            results.append((2, beyond, S[p, 2, beyond, :] - (lam * trace + (mu + mu) * dzs[2])))
+            results.append((4, beyond, S[p, 4, beyond, :] - (mu * (dzs[0] + dxs[2]))))
+            results.append((5, beyond, S[p, 5, beyond, :] - (mu * (dzs[1] + dy(near[2])))))
+
+        write(p, results)
 
         for i in range(2):
             @functools.partial(reach, i)
             def _(i=i):
                 arrived(ER.at[slot, p, i], e_recv.at[slot, p, i])
+        results = []
         for i, x in ((0, 0), (1, 7)):
             for j, z in ((0, 0), (1, 7)):
                 edge_x, edge_z = (ER[slot, p, i, j, k : k + 1, :] for k in range(2))
                 sign = jnp.where(z_there[j], (-1.0, 1.0)[j], 0.0)
                 outer = pl.ds(rows(z, (-1, 8)[i]), 1)
                 at_z, at_x = slice(z, z + 1), slice(x, x + 1)
-                S[p, 0, outer, :] -= LX[i, p, at_z, :] * (sign * edge_z)
-                S[p, 4, outer, :] -= MX[i, p, at_z, :] * (sign * edge_x)
+                results.append((0, outer, S[p, 0, outer, :] - (LX[i, p, at_z, :] * (sign * edge_z))))
+                results.append((4, outer, S[p, 4, outer, :] - (MX[i, p, at_z, :] * (sign * edge_x))))
                 outer = pl.ds(rows((-1, 8)[j], x), 1)
-                S[p, 2, outer, :] -= LZ[j, p, at_x, :] * (sides[i] * edge_x)
-                S[p, 4, outer, :] -= MZ[j, p, at_x, :] * (sides[i] * edge_z)
+                results.append((2, outer, S[p, 2, outer, :] - (LZ[j, p, at_x, :] * (sides[i] * edge_x))))
+                results.append((4, outer, S[p, 4, outer, :] - (MZ[j, p, at_x, :] * (sides[i] * edge_z))))
+        write(p, results)
 
     def each_part(then):
-        def body(p, carry):
+        for p in range(3):
             then(p)
-            return carry
-
-        lax.fori_loop(0, 3, body, 0)
 
     move(MIDDLE, 0, 0)
 
@@ -490,11 +503,8 @@
             arrived(XR0.at[i, 6:8], x_first_recv.at[2, i])
     border((LEFT, RIGHT))
 
-    def begin(p, carry):
-        move(p, 0, 0)
-        return carry
-
-    lax.fori_loop(1, 3, begin, 0)
+    move(LEFT, 0, 0)
+    move(RIGHT, 0, 0)
 
     arrived(ZR0.at[:, 8:12], z_first_recv.at[1])
     for i in range(2):

time: 44.9 us -> 44.9 us (level)
  no operation moved by 1% of the time
where the time goes in v3:
time: 44.9 us; the launch traced here: 44.8 us
  Pallas kernels  44 us (98%)
  local copies, waits for them, and re-layouts  0.82 us (2%)
    pallas_call x1, Pallas kernels, on_device(): pl.pallas_call(functools.partial(kernel, sizes), out_shape=jax.ShapeDtype...  44 us

profile of v3, /device:TPU:96, one launch (start us, length us, event | category | flops | bytes accessed | tf_op | source)
XLA Modules:
  0.0 44.8 jit_solution(15060617380928788805)
XLA Ops:
  0.0 44.0 %shard_map.73 = f32[9,8,8,256]{3,2,1,0:T(8,128)S(1)} custom-call(f32[9,8,8,256]{3,2,1,0:T(8,128)} %state_in.1, f32[6,8,256]{2,1,0:T(8,128)} %source_in.1, s32[8,256]{1,0:T(8,128)} %floor_in.1, s32[8,8,256]{2,1,0:T(8,128)} %region_in.1, f32[16]{0:T(128)} %lame_in.1, f32[16]{0:T(128)} %shear_in.1, f32[16]{0:T(128)} %buoy_in.1), custom_call_target="tpu_custom_call" | custom-call | tf_op jit(solution)/shard_map/pallas_call | solution.py:574
  44.0 0.8 %copy.9 = f32[9,8,8,256]{3,2,1,0:T(8,128)} copy(f32[9,8,8,256]{3,2,1,0:T(8,128)S(1)} %shard_map.73) | data formatting | bytes 1179648

commit v4 on v3

--- a/solution.py
+++ b/solution.py
@@ -284,22 +284,20 @@
     def z_base(p, s, last):
         return 12 + 18 * s + (3 * p if last else 6 * p)
 
-    def x_copy(p, i, s, slot, last):
-        n = 3 if last else 6
+    def x_copy(p, i, half, s, slot, last):
         return remote(
-            OX.at[i, pl.ds(x_base(p, s, last), n)], XR.at[slot, p, 1 - i, 0:n], x_send.at[i], x_recv.at[slot, p, 1 - i],
-            (0, sides[i], 0))
+            OX.at[i, pl.ds(x_base(p, s, last) + 3 * half, 3)], XR.at[slot, p, 1 - i, 3 * half : 3 * half + 3],
+            x_send.at[i], x_recv.at[slot, p, 1 - i], (0, sides[i], 0))
 
     def e_copy(p, i, j, s, slot):
         return remote(
             OE.at[i, 3 * s + p, j], ER.at[slot, p, 1 - i, 1 - j], e_send.at[i],
             e_recv.at[slot, p, 1 - i], (sides[j], sides[i], 0))
 
-    def z_copy(p, i, s, slot, last):
-        n = 3 if last else 6
+    def z_copy(p, i, half, s, slot, last):
         return remote(
-            OZ.at[i, pl.ds(z_base(p, s, last), n)], ZR.at[slot, p, 1 - i, 0:n], z_send.at[i], z_recv.at[slot, p],
-            (sides[i], 0, 0))
+            OZ.at[i, pl.ds(z_base(p, s, last) + 3 * half, 3)], ZR.at[slot, p, 1 - i, 3 * half : 3 * half + 3],
+            z_send.at[i], z_recv.at[slot, p], (sides[i], 0, 0))
 
     def move(p, s, slot, last=False):
         def accelerate(levels):
@@ -342,14 +340,16 @@
 
             @functools.partial(reach, i)
             def _(i=i):
-                x_copy(p, i, s, slot, last).start()
+                for half in (0,) if last else (0, 1):
+                    x_copy(p, i, half, s, slot, last).start()
         base = z_base(p, s, last)
         for i, (z, inner) in enumerate(((0, 1), (7, 6))):
             for f in range(3):
                 OZ[i, base + f] = V[p, f, level(z), :]
                 if not last:
                     OZ[i, base + 3 + f] = V[p, f, level(inner), :]
-            z_copy(p, i, s, slot, last).start()
+            for half in (0,) if last else (0, 1):
+                z_copy(p, i, half, s, slot, last).start()
 
         later = []
         for z in range(8):

time: 44.9 us -> 44.9 us (level)
  no operation moved by 1% of the time
where the time goes in v4:
time: 44.9 us; the launch traced here: 44.8 us
  Pallas kernels  44 us (98%)
  local copies, waits for them, and re-layouts  0.82 us (2%)
    pallas_call x1, Pallas kernels, on_device(): pl.pallas_call(functools.partial(kernel, sizes), out_shape=jax.ShapeDtype...  44 us

profile of v4, /device:TPU:96, one launch (start us, length us, event | category | flops | bytes accessed | tf_op | source)
XLA Modules:
  0.0 44.8 jit_solution(5014393068060523128)
XLA Ops:
  0.0 44.0 %shard_map.73 = f32[9,8,8,256]{3,2,1,0:T(8,128)S(1)} custom-call(f32[9,8,8,256]{3,2,1,0:T(8,128)} %state_in.1, f32[6,8,256]{2,1,0:T(8,128)} %source_in.1, s32[8,256]{1,0:T(8,128)} %floor_in.1, s32[8,8,256]{2,1,0:T(8,128)} %region_in.1, f32[16]{0:T(128)} %lame_in.1, f32[16]{0:T(128)} %shear_in.1, f32[16]{0:T(128)} %buoy_in.1), custom_call_target="tpu_custom_call" | custom-call | tf_op jit(solution)/shard_map/pallas_call | solution.py:574
  44.0 0.8 %copy.9 = f32[9,8,8,256]{3,2,1,0:T(8,128)} copy(f32[9,8,8,256]{3,2,1,0:T(8,128)S(1)} %shard_map.73) | data formatting | bytes 1179648

commit v5 on v3

--- a/solution.py
+++ b/solution.py
@@ -73,6 +73,17 @@
 
     def at(dz, dx, dyy):
         return (doms[dz], gxs[dx], gys[dyy])
+
+    odd = lax.rem(gx, 2) == 1
+    long_way = [there[0] & jnp.logical_not(odd), there[1] & odd]
+    short_way = [there[0] & odd, there[1] & jnp.logical_not(odd)]
+
+    def launch(then):
+        for way in (long_way, short_way):
+            for i in range(2):
+                @pl.when(way[i])
+                def _(i=i):
+                    then(i)
 
     def reach(i, then):
         pl.when(there[i])(then)
@@ -183,10 +194,10 @@
         OZ[i, 119] = side_by_side([source[s, :, cut(i)] for s in range(STEPS)] + [floor[:, cut(i)].astype(f32)], i)
 
     pl.semaphore_wait(barrier, 8 + 5 * (there[0].astype(jnp.int32) + there[1].astype(jnp.int32)))
-    for i in range(2):
-        @functools.partial(reach, i)
-        def _(i=i):
-            xa_first(i).start()
+    @launch
+    def _(i):
+        xa_first(i).start()
+
     for i in range(2):
         za_first(i).start()
         y_first(i).start()
@@ -227,7 +238,6 @@
         def _(i=i):
             for j in range(2):
                 xy_first(i, j).start()
-            xb_first(i).start()
     for i, z in ((0, 0), (1, 7)):
         parts = [[OZ[i, 2 * k + t] for t in range(2)] for k in range(3)]
         parts += [[m[p, pl.ds(8 * z, 8), :] for p in pair] for m in (L, M)]
@@ -237,7 +247,6 @@
         for j in range(2):
             OZ[i, 6 + j] = side_by_side([v[j] for v in parts], j)
             zy_first(i, j).start()
-        zb_first(i).start()
 
     left = (lane >= 128 - WIDE) & (gy > 0)
     right = (lane < WIDE) & (gy < n_gy - 1)
@@ -277,6 +286,12 @@
                 for p in parts:
                     S[p, f, level(z), :] = jnp.where(z_there[i], tiles[p], 0.0)
 
+    @launch
+    def _(i):
+        xb_first(i).start()
+
+    for i in range(2):
+        zb_first(i).start()
     border((MIDDLE,))
     def x_base(p, s, last):
         return 14 + 18 * s + (3 * p if last else 6 * p)
@@ -329,10 +344,12 @@
                     for k, f in enumerate((0, 2)):
                         OE[i, 3 * s + p, j, k : k + 1, :] = V[p, f, pl.ds(rows(7 * j, x), 1), :]
 
-                @functools.partial(reach, i)
-                def _(i=i):
-                    for j in range(2):
-                        e_copy(p, i, j, s, slot).start()
+
+            @launch
+            def _(i):
+                for j in range(2):
+                    e_copy(p, i, j, s, slot).start()
+
         accelerate((1, 2, 3))
         accelerate((4, 5, 6))
         base = x_base(p, s, last)
@@ -340,9 +357,10 @@
             for k, v in enumerate([V[p, f, column(c), :] for c in ((x,) if last else (x, inner)) for f in range(3)]):
                 OX[i, base + k] = v
 
-            @functools.partial(reach, i)
-            def _(i=i):
-                x_copy(p, i, s, slot, last).start()
+        @launch
+        def _(i):
+            x_copy(p, i, s, slot, last).start()
+
         base = z_base(p, s, last)
         for i, (z, inner) in enumerate(((0, 1), (7, 6))):
             for f in range(3):

time: 44.9 us -> 45.2 us (level)
  no operation moved by 1% of the time
where the time goes in v5:
time: 45.2 us; the launch traced here: 44.8 us
  Pallas kernels  44 us (97%)
  local copies, waits for them, and re-layouts  0.82 us (2%)
    pallas_call x1, Pallas kernels, on_device(): pl.pallas_call(functools.partial(kernel, sizes), out_shape=jax.ShapeDtype...  44 us

profile of v5, /device:TPU:96, one launch (start us, length us, event | category | flops | bytes accessed | tf_op | source)
XLA Modules:
  0.0 44.8 jit_solution(1003643651619977055)
XLA Ops:
  0.0 44.0 %shard_map.73 = f32[9,8,8,256]{3,2,1,0:T(8,128)S(1)} custom-call(f32[9,8,8,256]{3,2,1,0:T(8,128)} %state_in.1, f32[6,8,256]{2,1,0:T(8,128)} %source_in.1, s32[8,256]{1,0:T(8,128)} %floor_in.1, s32[8,8,256]{2,1,0:T(8,128)} %region_in.1, f32[16]{0:T(128)} %lame_in.1, f32[16]{0:T(128)} %shear_in.1, f32[16]{0:T(128)} %buoy_in.1), custom_call_target="tpu_custom_call" | custom-call | tf_op jit(solution)/shard_map/pallas_call | solution.py:592
  44.0 0.8 %copy.9 = f32[9,8,8,256]{3,2,1,0:T(8,128)} copy(f32[9,8,8,256]{3,2,1,0:T(8,128)S(1)} %shard_map.73) | data formatting | bytes 1179648

commit v6 on v3

--- a/solution.py
+++ b/solution.py
@@ -351,6 +351,7 @@
                     OZ[i, base + 3 + f] = V[p, f, level(inner), :]
             z_copy(p, i, s, slot, last).start()
 
+    def settle(p):
         later = []
         for z in range(8):
             own = level(z)
@@ -471,6 +472,7 @@
             then(p)
 
     move(MIDDLE, 0, 0)
+    settle(MIDDLE)
 
     arrived(YR, y_recv.at[0])
     low, high = YR[0, 8], YR[1, 8]
@@ -503,8 +505,10 @@
             arrived(XR0.at[i, 6:8], x_first_recv.at[2, i])
     border((LEFT, RIGHT))
 
-    move(LEFT, 0, 0)
-    move(RIGHT, 0, 0)
+    for p in (LEFT, RIGHT):
+        move(p, 0, 0)
+    for p in (LEFT, RIGHT):
+        settle(p)
 
     arrived(ZR0.at[:, 8:12], z_first_recv.at[1])
     for i in range(2):
@@ -529,6 +533,7 @@
             move(p, s, slot)
 
         each_part(turn)
+        each_part(settle)
         return carry
 
     lax.fori_loop(1, STEPS - 1, step, 0)
@@ -540,6 +545,7 @@
         move(p, end, end % 2, last=True)
 
     each_part(final)
+    each_part(settle)
 
     def gather(f, ref, k):
         for z in range(8):

time: 44.9 us -> 44.9 us (level)
  no operation moved by 1% of the time
where the time goes in v6:
time: 44.9 us; the launch traced here: 44.8 us
  Pallas kernels  44 us (98%)
  local copies, waits for them, and re-layouts  0.82 us (2%)
    pallas_call x1, Pallas kernels, on_device(): pl.pallas_call(functools.partial(kernel, sizes), out_shape=jax.ShapeDtype...  44 us

profile of v6, /device:TPU:96, one launch (start us, length us, event | category | flops | bytes accessed | tf_op | source)
XLA Modules:
  0.0 44.8 jit_solution(332051495184582081)
XLA Ops:
  0.0 44.0 %shard_map.73 = f32[9,8,8,256]{3,2,1,0:T(8,128)S(1)} custom-call(f32[9,8,8,256]{3,2,1,0:T(8,128)} %state_in.1, f32[6,8,256]{2,1,0:T(8,128)} %source_in.1, s32[8,256]{1,0:T(8,128)} %floor_in.1, s32[8,8,256]{2,1,0:T(8,128)} %region_in.1, f32[16]{0:T(128)} %lame_in.1, f32[16]{0:T(128)} %shear_in.1, f32[16]{0:T(128)} %buoy_in.1), custom_call_target="tpu_custom_call" | custom-call | tf_op jit(solution)/shard_map/pallas_call | solution.py:580
  44.0 0.8 %copy.9 = f32[9,8,8,256]{3,2,1,0:T(8,128)} copy(f32[9,8,8,256]{3,2,1,0:T(8,128)S(1)} %shard_map.73) | data formatting | bytes 1179648

commit v7 on v3

--- a/solution.py
+++ b/solution.py
@@ -10,6 +10,8 @@
 STEPS = 6
 COURANT = 0.25
 REGIONS = 16
+NEED = 106
+SPARE = 128 - NEED
 BLOCK = 16
 WIDE = 12
 MIDDLE, LEFT, RIGHT = 0, 1, 2
@@ -278,14 +280,26 @@
                     S[p, f, level(z), :] = jnp.where(z_there[i], tiles[p], 0.0)
 
     border((MIDDLE,))
+    def place(p):
+        return (lane + (52 - 42 * p)) & 127
+
+    def squeeze(where, row, k, sixth):
+        return jnp.where(where < NEED, row, pltpu.roll(sixth, NEED - SPARE * k, 1))
+
+    def restore(where, tiles):
+        sixth = pltpu.roll(tiles[4], 5 * SPARE, 1)
+        for k in range(4):
+            sixth = jnp.where((where >= SPARE * k) & (where < SPARE * (k + 1)), pltpu.roll(tiles[k], SPARE * (k + 1), 1), sixth)
+        return sixth
+
     def x_base(p, s, last):
-        return 14 + 18 * s + (3 * p if last else 6 * p)
+        return 14 + 15 * s + (3 * p if last else 5 * p)
 
     def z_base(p, s, last):
         return 12 + 18 * s + (3 * p if last else 6 * p)
 
     def x_copy(p, i, s, slot, last):
-        n = 3 if last else 6
+        n = 3 if last else 5
         return remote(
             OX.at[i, pl.ds(x_base(p, s, last), n)], XR.at[slot, p, 1 - i, 0:n], x_send.at[i], x_recv.at[slot, p, 1 - i],
             (0, sides[i], 0))
@@ -337,7 +351,14 @@
         accelerate((4, 5, 6))
         base = x_base(p, s, last)
         for i, (x, inner) in enumerate(((0, 1), (7, 6))):
-            for k, v in enumerate([V[p, f, column(c), :] for c in ((x,) if last else (x, inner)) for f in range(3)]):
+            near = [V[p, f, column(x), :] for f in range(3)]
+            if last:
+                tiles_out = near
+            else:
+                far = [V[p, f, column(inner), :] for f in range(3)]
+                where = place(p)
+                tiles_out = [squeeze(where, v, k, far[1]) for k, v in enumerate(near + [far[0], far[2]])]
+            for k, v in enumerate(tiles_out):
                 OX[i, base + k] = v
 
             @functools.partial(reach, i)
@@ -420,7 +441,8 @@
             write(p, results)
             return
         for i, x, sign in ((0, 0, -1.0), (1, 7, 1.0)):
-            near, far = [XR[slot, p, i, f] for f in range(3)], [XR[slot, p, i, 3 + f] for f in range(3)]
+            got = [XR[slot, p, i, k] for k in range(5)]
+            near, far = got[0:3], (got[3], restore(place(p), got), got[4])
             lam, mu = LX[i, p], MX[i, p]
             dxs = [sign * (far[f] - V[p, f, column(x), :]) for f in range(3)]
             dzs = {}
@@ -595,13 +617,13 @@
                 tiles(2, 3),
                 tiles(2, 3),
                 tiles(2, 3),
-                tiles(2, 113),
+                tiles(2, 98),
                 tiles(2, 120),
                 pltpu.VMEM((2, 3 * STEPS - 3, 2, 2, 128), f32),
                 tiles(2, 14),
                 tiles(2, 12),
                 tiles(2, 9),
-                tiles(2, 3, 2, 6),
+                tiles(2, 3, 2, 5),
                 tiles(2, 3, 2, 6),
                 pltpu.VMEM((2, 3, 2, 2, 2, 128), f32),
                 pltpu.SemaphoreType.DMA((7,)),

time: 44.9 us -> 44.9 us (level)
  no operation moved by 1% of the time
where the time goes in v7:
time: 44.9 us; the launch traced here: 44.7 us
  Pallas kernels  43.9 us (98%)
  local copies, waits for them, and re-layouts  0.82 us (2%)
    pallas_call x1, Pallas kernels, on_device(): pl.pallas_call(functools.partial(kernel, sizes), out_shape=jax.ShapeDtype...  43.9 us

profile of v7, /device:TPU:96, one launch (start us, length us, event | category | flops | bytes accessed | tf_op | source)
XLA Modules:
  0.0 44.7 jit_solution(15253053970268224413)
XLA Ops:
  0.0 43.9 %shard_map.73 = f32[9,8,8,256]{3,2,1,0:T(8,128)S(1)} custom-call(f32[9,8,8,256]{3,2,1,0:T(8,128)} %state_in.1, f32[6,8,256]{2,1,0:T(8,128)} %source_in.1, s32[8,256]{1,0:T(8,128)} %floor_in.1, s32[8,8,256]{2,1,0:T(8,128)} %region_in.1, f32[16]{0:T(128)} %lame_in.1, f32[16]{0:T(128)} %shear_in.1, f32[16]{0:T(128)} %buoy_in.1), custom_call_target="tpu_custom_call" | custom-call | tf_op jit(solution)/shard_map/pallas_call | solution.py:596
  43.9 0.8 %copy.9 = f32[9,8,8,256]{3,2,1,0:T(8,128)} copy(f32[9,8,8,256]{3,2,1,0:T(8,128)S(1)} %shard_map.73) | data formatting | bytes 1179648

commit v8 on v3

--- a/solution.py
+++ b/solution.py
@@ -57,7 +57,8 @@
     loads = [
         pltpu.make_async_copy(src, dst, in_sem.at[i])
         for i, (src, dst) in enumerate((
-            (region_in, region), (floor_in, floor), (source_in, source), (state_in, state),
+            (floor_in, floor), (state_in.at[3:6], state.at[3:6]), (state_in.at[6:9], state.at[6:9]),
+            (state_in.at[0:3], state.at[0:3]), (region_in, region), (source_in, source),
             (lame_in, lame), (shear_in, shear), (buoy_in, buoy)))
     ]
     for load in loads:
@@ -106,7 +107,7 @@
             for z in (-1, 8):
                 V[p, f, level(z), :] = zero
 
-    for load in loads[:4]:
+    for load in loads[:6]:
         load.wait()
 
     def side_by_side(parts, t):
@@ -182,16 +183,7 @@
                 [state[f, z, :, cut(i)] for f in range(9)] + [region[z, :, cut(i)].astype(f32)], i)
         OZ[i, 119] = side_by_side([source[s, :, cut(i)] for s in range(STEPS)] + [floor[:, cut(i)].astype(f32)], i)
 
-    pl.semaphore_wait(barrier, 8 + 5 * (there[0].astype(jnp.int32) + there[1].astype(jnp.int32)))
-    for i in range(2):
-        @functools.partial(reach, i)
-        def _(i=i):
-            xa_first(i).start()
-    for i in range(2):
-        za_first(i).start()
-        y_first(i).start()
-
-    for load in loads[4:]:
+    for load in loads[6:]:
         load.wait()
     scale = 0.5 * COURANT
     tables = [[t[k] * scale for k in range(REGIONS)] for t in (lame, shear, buoy)]
@@ -209,8 +201,6 @@
         made = [materials(region[z, :, cut(t)], floor[:, cut(t)], z) for t in range(2)]
         for k, ref in enumerate((L, M, B)):
             put(ref, (pl.ds(8 * z, 8), everywhere), [m[k] for m in made])
-        for f in range(3):
-            put(V, (f, level(z), everywhere), [state[f, z, :, cut(t)] for t in range(2)])
 
     for i, x in ((0, 0), (1, 7)):
         parts = [[OX[i, 2 * k + t] for t in range(2)] for k in range(3)]
@@ -222,12 +212,6 @@
                 OX[i, 2 * k + t + 2] = parts[k][t]
         for j in range(2):
             OX[i, 6 + j] = side_by_side([v[j] for v in parts], j)
-
-        @functools.partial(reach, i)
-        def _(i=i):
-            for j in range(2):
-                xy_first(i, j).start()
-            xb_first(i).start()
     for i, z in ((0, 0), (1, 7)):
         parts = [[OZ[i, 2 * k + t] for t in range(2)] for k in range(3)]
         parts += [[m[p, pl.ds(8 * z, 8), :] for p in pair] for m in (L, M)]
@@ -236,8 +220,27 @@
                 OZ[i, 2 * k + t + 2] = parts[k][t]
         for j in range(2):
             OZ[i, 6 + j] = side_by_side([v[j] for v in parts], j)
+
+    pl.semaphore_wait(barrier, 8 + 5 * (there[0].astype(jnp.int32) + there[1].astype(jnp.int32)))
+    for i in range(2):
+        @functools.partial(reach, i)
+        def _(i=i):
+            for j in range(2):
+                xy_first(i, j).start()
+            xa_first(i).start()
+    for i in range(2):
+        for j in range(2):
             zy_first(i, j).start()
+        za_first(i).start()
+        y_first(i).start()
+    for i in range(2):
+        @functools.partial(reach, i)
+        def _(i=i):
+            xb_first(i).start()
         zb_first(i).start()
+    for z in range(8):
+        for f in range(3):
+            put(V, (f, level(z), everywhere), [state[f, z, :, cut(t)] for t in range(2)])
 
     left = (lane >= 128 - WIDE) & (gy > 0)
     right = (lane < WIDE) & (gy < n_gy - 1)
@@ -604,7 +607,7 @@
                 tiles(2, 3, 2, 6),
                 tiles(2, 3, 2, 6),
                 pltpu.VMEM((2, 3, 2, 2, 2, 128), f32),
-                pltpu.SemaphoreType.DMA((7,)),
+                pltpu.SemaphoreType.DMA((9,)),
                 pltpu.SemaphoreType.DMA((2,)),
                 pltpu.SemaphoreType.DMA((2,)),
                 pltpu.SemaphoreType.DMA((2,)),

time: 44.9 us -> 45.2 us (level)
  no operation moved by 1% of the time
where the time goes in v8:
time: 45.2 us; the launch traced here: 44.9 us
  Pallas kernels  44.1 us (98%)
  local copies, waits for them, and re-layouts  0.82 us (2%)
    pallas_call x1, Pallas kernels, on_device(): pl.pallas_call(functools.partial(kernel, sizes), out_shape=jax.ShapeDtype...  44.1 us

profile of v8, /device:TPU:96, one launch (start us, length us, event | category | flops | bytes accessed | tf_op | source)
XLA Modules:
  0.0 44.9 jit_solution(13834684507962957851)
XLA Ops:
  0.0 44.1 %shard_map.73 = f32[9,8,8,256]{3,2,1,0:T(8,128)S(1)} custom-call(f32[9,8,8,256]{3,2,1,0:T(8,128)} %state_in.1, f32[6,8,256]{2,1,0:T(8,128)} %source_in.1, s32[8,256]{1,0:T(8,128)} %floor_in.1, s32[8,8,256]{2,1,0:T(8,128)} %region_in.1, f32[16]{0:T(128)} %lame_in.1, f32[16]{0:T(128)} %shear_in.1, f32[16]{0:T(128)} %buoy_in.1), custom_call_target="tpu_custom_call" | custom-call | tf_op jit(solution)/shard_map/pallas_call | solution.py:577
  44.1 0.8 %copy.9 = f32[9,8,8,256]{3,2,1,0:T(8,128)} copy(f32[9,8,8,256]{3,2,1,0:T(8,128)S(1)} %shard_map.73) | data formatting | bytes 1179648

commit v9 on v3

--- a/solution.py
+++ b/solution.py
@@ -57,7 +57,8 @@
     loads = [
         pltpu.make_async_copy(src, dst, in_sem.at[i])
         for i, (src, dst) in enumerate((
-            (region_in, region), (floor_in, floor), (source_in, source), (state_in, state),
+            (floor_in, floor), (source_in, source), (state_in.at[3:9], state.at[3:9]),
+            (state_in.at[0:3], state.at[0:3]), (region_in, region),
             (lame_in, lame), (shear_in, shear), (buoy_in, buoy)))
     ]
     for load in loads:
@@ -106,7 +107,7 @@
             for z in (-1, 8):
                 V[p, f, level(z), :] = zero
 
-    for load in loads[:4]:
+    for load in loads[:3]:
         load.wait()
 
     def side_by_side(parts, t):
@@ -176,23 +177,23 @@
             for t in range(2):
                 OX[i, 2 * k + t] = S[pair[t], x_fields[k], column(at_edge), :]
                 OZ[i, 2 * k + t] = S[pair[t], z_fields[k], level(at_edge), :]
+    pl.semaphore_wait(barrier, 8 + 5 * (there[0].astype(jnp.int32) + there[1].astype(jnp.int32)))
+    for i in range(2):
+        @functools.partial(reach, i)
+        def _(i=i):
+            xa_first(i).start()
+        za_first(i).start()
+    for load in loads[3:]:
+        load.wait()
     for i in range(2):
         for z in range(8):
             OZ[i, 111 + z] = side_by_side(
                 [state[f, z, :, cut(i)] for f in range(9)] + [region[z, :, cut(i)].astype(f32)], i)
         OZ[i, 119] = side_by_side([source[s, :, cut(i)] for s in range(STEPS)] + [floor[:, cut(i)].astype(f32)], i)
 
-    pl.semaphore_wait(barrier, 8 + 5 * (there[0].astype(jnp.int32) + there[1].astype(jnp.int32)))
-    for i in range(2):
-        @functools.partial(reach, i)
-        def _(i=i):
-            xa_first(i).start()
-    for i in range(2):
-        za_first(i).start()
+    for i in range(2):
         y_first(i).start()
 
-    for load in loads[4:]:
-        load.wait()
     scale = 0.5 * COURANT
     tables = [[t[k] * scale for k in range(REGIONS)] for t in (lame, shear, buoy)]
 
@@ -604,7 +605,7 @@
                 tiles(2, 3, 2, 6),
                 tiles(2, 3, 2, 6),
                 pltpu.VMEM((2, 3, 2, 2, 2, 128), f32),
-                pltpu.SemaphoreType.DMA((7,)),
+                pltpu.SemaphoreType.DMA((8,)),
                 pltpu.SemaphoreType.DMA((2,)),
                 pltpu.SemaphoreType.DMA((2,)),
                 pltpu.SemaphoreType.DMA((2,)),

time: 44.9 us -> 45.1 us (level)
  no operation moved by 1% of the time
where the time goes in v9:
time: 45.1 us; the launch traced here: 44.8 us
  Pallas kernels  44 us (98%)
  local copies, waits for them, and re-layouts  0.82 us (2%)
    pallas_call x1, Pallas kernels, on_device(): pl.pallas_call(functools.partial(kernel, sizes), out_shape=jax.ShapeDtype...  44 us

profile of v9, /device:TPU:96, one launch (start us, length us, event | category | flops | bytes accessed | tf_op | source)
XLA Modules:
  0.0 44.8 jit_solution(17698381406484454780)
XLA Ops:
  0.0 44.0 %shard_map.73 = f32[9,8,8,256]{3,2,1,0:T(8,128)S(1)} custom-call(f32[9,8,8,256]{3,2,1,0:T(8,128)} %state_in.1, f32[6,8,256]{2,1,0:T(8,128)} %source_in.1, s32[8,256]{1,0:T(8,128)} %floor_in.1, s32[8,8,256]{2,1,0:T(8,128)} %region_in.1, f32[16]{0:T(128)} %lame_in.1, f32[16]{0:T(128)} %shear_in.1, f32[16]{0:T(128)} %buoy_in.1), custom_call_target="tpu_custom_call" | custom-call | tf_op jit(solution)/shard_map/pallas_call | solution.py:575
  44.0 0.8 %copy.9 = f32[9,8,8,256]{3,2,1,0:T(8,128)} copy(f32[9,8,8,256]{3,2,1,0:T(8,128)S(1)} %shard_map.73) | data formatting | bytes 1179648

commit v10 on v3

--- a/solution.py
+++ b/solution.py
@@ -57,7 +57,8 @@
     loads = [
         pltpu.make_async_copy(src, dst, in_sem.at[i])
         for i, (src, dst) in enumerate((
-            (region_in, region), (floor_in, floor), (source_in, source), (state_in, state),
+            (region_in, region), (floor_in, floor), (source_in, source),
+            (state_in.at[0:3], state.at[0:3]), (state_in.at[3:6], state.at[3:6]), (state_in.at[6:9], state.at[6:9]),
             (lame_in, lame), (shear_in, shear), (buoy_in, buoy)))
     ]
     for load in loads:
@@ -106,7 +107,7 @@
             for z in (-1, 8):
                 V[p, f, level(z), :] = zero
 
-    for load in loads[:4]:
+    for load in loads[:6]:
         load.wait()
 
     def side_by_side(parts, t):
@@ -191,7 +192,7 @@
         za_first(i).start()
         y_first(i).start()
 
-    for load in loads[4:]:
+    for load in loads[6:]:
         load.wait()
     scale = 0.5 * COURANT
     tables = [[t[k] * scale for k in range(REGIONS)] for t in (lame, shear, buoy)]
@@ -604,7 +605,7 @@
                 tiles(2, 3, 2, 6),
                 tiles(2, 3, 2, 6),
                 pltpu.VMEM((2, 3, 2, 2, 2, 128), f32),
-                pltpu.SemaphoreType.DMA((7,)),
+                pltpu.SemaphoreType.DMA((9,)),
                 pltpu.SemaphoreType.DMA((2,)),
                 pltpu.SemaphoreType.DMA((2,)),
                 pltpu.SemaphoreType.DMA((2,)),

time: 44.9 us -> 44.9 us (level)
  no operation moved by 1% of the time
where the time goes in v10:
time: 44.9 us; the launch traced here: 44.8 us
  Pallas kernels  44 us (98%)
  local copies, waits for them, and re-layouts  0.82 us (2%)
    pallas_call x1, Pallas kernels, on_device(): pl.pallas_call(functools.partial(kernel, sizes), out_shape=jax.ShapeDtype...  44 us

profile of v10, /device:TPU:96, one launch (start us, length us, event | category | flops | bytes accessed | tf_op | source)
XLA Modules:
  0.0 44.8 jit_solution(17282040658838432389)
XLA Ops:
  0.0 44.0 %shard_map.73 = f32[9,8,8,256]{3,2,1,0:T(8,128)S(1)} custom-call(f32[9,8,8,256]{3,2,1,0:T(8,128)} %state_in.1, f32[6,8,256]{2,1,0:T(8,128)} %source_in.1, s32[8,256]{1,0:T(8,128)} %floor_in.1, s32[8,8,256]{2,1,0:T(8,128)} %region_in.1, f32[16]{0:T(128)} %lame_in.1, f32[16]{0:T(128)} %shear_in.1, f32[16]{0:T(128)} %buoy_in.1), custom_call_target="tpu_custom_call" | custom-call | tf_op jit(solution)/shard_map/pallas_call | solution.py:575
  44.0 0.8 %copy.9 = f32[9,8,8,256]{3,2,1,0:T(8,128)} copy(f32[9,8,8,256]{3,2,1,0:T(8,128)S(1)} %shard_map.73) | data formatting | bytes 1179648
